TPU v7x, 32 devices: a whole 2x2x4 slice. The times are simulated.
32 devices in a mesh: grp: 8 (over z, x), kin: 4 (over y, core).
Axes of the slice: x: 2, y: 2, z: 4, core: 2. Of those that a mesh axis runs over, the one named last changes fastest.
Arguments:
- waves: bfloat16 [32, 2, 8, 1024], P(('grp', 'kin')), may hold values from -6 to 6
- vector: float32 [32, 2, 16], P(('grp', 'kin')), may hold values from -6 to 6
- energies: float32 [32, 16], P(('grp', 'kin')), may hold values from 0.5 to 1.5
- basis: bfloat16 [2, 1024, 1536], replicated, may hold values from -0.1875 to 0.1875
- screening: float32 [32, 1536], replicated, may hold values from 0.05 to 1
- coulomb: float32 [1536], replicated, may hold values from 0.01 to 0.2
- qmap: int32 [32, 32], P(('grp', 'kin')), may hold values from 0 to 31, as said below
Outputs:
- applied: float32 [32, 2, 16], P(('grp', 'kin'))
Inputs may be any that keep to these rules, and one draw needn't show every extreme that they name: qmap[s, s2] is the index, on the periodic 8 x 4 k-grid, of the difference of the grid points of the stored k-points s and s2 (grid point x * 4 + y); the stored k-points are a permutation of the grid points, so each row holds every value once.
All inputs are finite; a program needn't handle non-finite values.
Results may differ from a plain program's by a relative error of at most 0.0057.
Values may be sent and summed in bfloat16 or wider, within the bound.
A program may use at most 64 MiB of HBM per device.

v0:
```python
import jax
import jax.numpy as jnp
from jax import lax
from jax.sharding import PartitionSpec as P

NV = 4
NC = 4
NT = 16


def shifted(value, axis, steps):
    count = lax.axis_size(axis)
    pairs = [(source, (source + steps) % count) for source in range(count)]
    return lax.ppermute(value, axis, pairs)


def conj_products(left, right):
    left_re = left[:, 0].astype(jnp.float32)[:, None, :, None, :]
    left_im = left[:, 1].astype(jnp.float32)[:, None, :, None, :]
    right_re = right[:, 0].astype(jnp.float32)[None, :, None, :, :]
    right_im = right[:, 1].astype(jnp.float32)[None, :, None, :, :]
    real_part = (left_re * right_re + left_im * right_im).astype(jnp.bfloat16)
    imag_part = (left_re * right_im - left_im * right_re).astype(jnp.bfloat16)
    return (real_part, imag_part)


def densities(pair_re, pair_im, basis):
    rows = pair_re.shape[0]
    stacked = jnp.concatenate([pair_re, pair_im], 0)
    first = jnp.dot(stacked, basis[0], preferred_element_type=jnp.float32)
    second = jnp.dot(stacked, basis[1], preferred_element_type=jnp.float32)
    real_part = (first[:rows] - second[rows:]).astype(jnp.bfloat16)
    imag_part = (second[:rows] + first[rows:]).astype(jnp.bfloat16)
    return (real_part, imag_part)


def block_terms(own_waves, own_vector, part_waves, part_vector, weights, basis):
    highest = lax.Precision.HIGHEST
    owners = own_waves.shape[0]
    partners = part_waves.shape[0]
    points = own_waves.shape[3]
    cond_re, cond_im = conj_products(own_waves[:, :, NV:], part_waves[:, :, NV:])
    val_re, val_im = conj_products(own_waves[:, :, :NV], part_waves[:, :, :NV])
    pair_re = jnp.concatenate(
        [
            cond_re.reshape(owners, partners, NC * NC, points),
            val_re.reshape(owners, partners, NV * NV, points),
        ],
        2,
    ).reshape(-1, points)
    pair_im = jnp.concatenate(
        [
            cond_im.reshape(owners, partners, NC * NC, points),
            val_im.reshape(owners, partners, NV * NV, points),
        ],
        2,
    ).reshape(-1, points)
    dens_re, dens_im = densities(pair_re, pair_im, basis)
    dens_re = dens_re.reshape(owners, partners, NC * NC + NV * NV, -1)
    dens_im = dens_im.reshape(owners, partners, NC * NC + NV * NV, -1)
    wcond_re = dens_re[:, :, : NC * NC].astype(jnp.float32) * weights[:, :, None, :]
    wcond_im = dens_im[:, :, : NC * NC].astype(jnp.float32) * weights[:, :, None, :]
    val_dre = dens_re[:, :, NC * NC :].astype(jnp.float32)
    val_dim = dens_im[:, :, NC * NC :].astype(jnp.float32)
    kern_re = jnp.einsum("abpg,abqg->abpq", wcond_re, val_dre, precision=highest) + jnp.einsum(
        "abpg,abqg->abpq", wcond_im, val_dim, precision=highest
    )
    kern_im = jnp.einsum("abpg,abqg->abpq", wcond_re, val_dim, precision=highest) - jnp.einsum(
        "abpg,abqg->abpq", wcond_im, val_dre, precision=highest
    )
    kern_re = kern_re.reshape(owners, partners, NC, NC, NV, NV)
    kern_im = kern_im.reshape(owners, partners, NC, NC, NV, NV)
    own_x = own_vector.astype(jnp.float32).reshape(owners, 2, NV, NC)
    part_x = part_vector.astype(jnp.float32).reshape(partners, 2, NV, NC)
    form_d = "abcdvw,bwd->avc"
    direct_re = jnp.einsum(form_d, kern_re, part_x[:, 0], precision=highest) - jnp.einsum(
        form_d, kern_im, part_x[:, 1], precision=highest
    )
    direct_im = jnp.einsum(form_d, kern_re, part_x[:, 1], precision=highest) + jnp.einsum(
        form_d, kern_im, part_x[:, 0], precision=highest
    )
    form_h = "abcdvw,avc->bwd"
    herm_re = jnp.einsum(form_h, kern_re, own_x[:, 0], precision=highest) + jnp.einsum(
        form_h, kern_im, own_x[:, 1], precision=highest
    )
    herm_im = jnp.einsum(form_h, kern_re, own_x[:, 1], precision=highest) - jnp.einsum(
        form_h, kern_im, own_x[:, 0], precision=highest
    )
    direct = jnp.stack([direct_re.reshape(owners, NT), direct_im.reshape(owners, NT)], 1)
    hermitian = jnp.stack([herm_re.reshape(partners, NT), herm_im.reshape(partners, NT)], 1)
    return (direct, hermitian)


def own_densities(waves, basis):
    count = waves.shape[0]
    points = waves.shape[3]
    val_re = waves[:, 0, :NV].astype(jnp.float32)[:, :, None, :]
    val_im = waves[:, 1, :NV].astype(jnp.float32)[:, :, None, :]
    con_re = waves[:, 0, NV:].astype(jnp.float32)[:, None, :, :]
    con_im = waves[:, 1, NV:].astype(jnp.float32)[:, None, :, :]
    pair_re = (val_re * con_re + val_im * con_im).astype(jnp.bfloat16).reshape(-1, points)
    pair_im = (val_re * con_im - val_im * con_re).astype(jnp.bfloat16).reshape(-1, points)
    dens_re, dens_im = densities(pair_re, pair_im, basis)
    return (dens_re.reshape(count, NT, -1), dens_im.reshape(count, NT, -1))


def on_device(waves, vector, energies, basis, screening, coulomb, qmap):
    highest = lax.Precision.HIGHEST
    groups = lax.axis_size("grp")
    members = lax.axis_size("kin")
    offset = groups // 4
    own_count = waves.shape[0]
    block = own_count * members
    total = block * groups
    coarse = vector.astype(jnp.bfloat16)
    group_waves, group_vector = (
        lax.all_gather(waves, "kin", axis=0, tiled=True),
        lax.all_gather(coarse, "kin", axis=0, tiled=True),
    )
    partner_waves, partner_vector = shifted((group_waves, group_vector), "grp", offset)
    partner_group = (lax.axis_index("grp") - offset) % groups
    qrows = lax.dynamic_slice_in_dim(qmap, partner_group * block, block, 1)
    weights = jnp.take(screening, qrows.reshape(-1), axis=0).reshape(own_count, block, -1)
    direct, hermitian = block_terms(waves, coarse, partner_waves, partner_vector, weights, basis)
    ex_re, ex_im = own_densities(waves, basis)
    ex_re = ex_re.astype(jnp.float32)
    ex_im = ex_im.astype(jnp.float32)
    coarse_x = coarse.astype(jnp.float32)
    part_re = jnp.einsum("atg,at->g", ex_re, coarse_x[:, 0], precision=highest) - jnp.einsum(
        "atg,at->g", ex_im, coarse_x[:, 1], precision=highest
    )
    part_im = jnp.einsum("atg,at->g", ex_re, coarse_x[:, 1], precision=highest) + jnp.einsum(
        "atg,at->g", ex_im, coarse_x[:, 0], precision=highest
    )
    sum_re, sum_im = lax.psum((part_re, part_im), ("grp", "kin"))
    pot_re = coulomb * sum_re
    pot_im = coulomb * sum_im
    exch_re = jnp.einsum("atg,g->at", ex_re, pot_re, precision=highest) + jnp.einsum(
        "atg,g->at", ex_im, pot_im, precision=highest
    )
    exch_im = jnp.einsum("atg,g->at", ex_re, pot_im, precision=highest) - jnp.einsum(
        "atg,g->at", ex_im, pot_re, precision=highest
    )
    exchange = jnp.stack([exch_re, exch_im], 1)
    summed = lax.psum_scatter(hermitian, "kin", scatter_dimension=0, tiled=True)
    returned = shifted(summed, "grp", -offset)
    scale = jnp.float32(1.0 / total)
    return energies[:, None, :] * vector + 2.0 * scale * exchange - scale * (direct + returned)


def solution(mesh):
    return jax.shard_map(
        on_device,
        mesh=mesh,
        in_specs=(
            P(("grp", "kin"), None, None, None),
            P(("grp", "kin"), None, None),
            P(("grp", "kin"), None),
            P(),
            P(),
            P(),
            P(("grp", "kin"), None),
        ),
        out_specs=P(("grp", "kin"), None, None),
        check_vma=False,
    )
```

profile of v0, /device:TPU:0, one launch (start us, length us, event | category | flops | bytes accessed | tf_op | source)
XLA Modules:
  0.0 90.4 jit_solution(5716294400683144207)
XLA Ops:
  0.0 6.8 %all_gather.6 = bf16[4,2,8,1024]{3,2,1,0:T(8,128)(2,1)S(1)} all-gather(bf16[1,2,8,1024]{3,2,1,0:T(8,128)(2,1)} %param.7), channel_id=1, replica_groups=mesh['grp'=8,'kin'=4] {'kin'}, dimensions={0}, use_global_device_ids=true | all-gather | bytes 163840 | tf_op jit(solution)/shard_map/all_gather | solution.py:117
  6.8 1.9 %collective-permute-start = (bf16[4,2,8,1024]{3,2,1,0:T(8,128)(2,1)S(1)}, bf16[4,2,8,1024]{3,2,1,0:T(8,128)(2,1)S(1)}, u32[]{:S(2)}, u32[]{:S(2)}) collective-permute-start(bf16[4,2,8,1024]{3,2,1,0:T(8,128)(2,1)S(1)} %all_gather.6), channel_id=1, source_target_pairs={{0,8},{4,12},{8,16},{12,20},{16,24},{20,28},{24,0},{28,4},{1,9},{5... | collective-permute-start | bytes 393224 | tf_op jit(solution)/shard_map/ppermute | solution.py:14
  8.8 0.7 convert_element_type.197
  9.5 5.0 %all_gather.7 = bf16[4,2,16]{2,1,0:T(2,128)(2,1)S(1)} all-gather(bf16[1,2,16]{2,1,0:T(2,128)(2,1)S(1)} %convert_element_type.197), channel_id=1, replica_groups=mesh['grp'=8,'kin'=4] {'kin'}, dimensions={0}, use_global_device_ids=true | all-gather | bytes 320 | tf_op jit(solution)/shard_map/all_gather | solution.py:118
  14.5 1.6 %collective-permute-start.1 = (bf16[4,2,16]{2,1,0:T(2,128)(2,1)S(1)}, bf16[4,2,16]{2,1,0:T(2,128)(2,1)S(1)}, u32[]{:S(2)}, u32[]{:S(2)}) collective-permute-start(bf16[4,2,16]{2,1,0:T(2,128)(2,1)S(1)} %all_gather.7), channel_id=1, source_target_pairs={{0,8},{4,12},{8,16},{12,20},{16,24},{20,28},{24,0},{28,4},{1,9},{5... | collective-permute-start | bytes 776 | tf_op jit(solution)/shard_map/ppermute | solution.py:14
  16.1 0.8 bitcast_convert_fusion.2
  17.1 2.5 %fusion.2 = f32[32,1536]{1,0:T(8,128)S(1)} fusion(bf16[2,1024,1536]{2,1,0:T(8,128)(2,1)} %param.10, bf16[16,1024]{1,0:T(8,128)(2,1)S(1)} %get-tuple-element.22, bf16[16,1024]{1,0:T(8,128)(2,1)S(1)} %get-tuple-element.21), kind=kOutput, calls=%fused_computation.3 | convolution fusion | flops 100794368 | bytes 3407872 | tf_op jit(solution)/shard_map/dot_general | solution.py:31
  19.7 2.5 %fusion.6 = f32[32,1536]{1,0:T(8,128)S(1)} fusion(bf16[2,1024,1536]{2,1,0:T(8,128)(2,1)} %param.10, bf16[16,1024]{1,0:T(8,128)(2,1)S(1)} %get-tuple-element.22, bf16[16,1024]{1,0:T(8,128)(2,1)S(1)} %get-tuple-element.21), kind=kOutput, calls=%fused_computation.7 | convolution fusion | flops 100794368 | bytes 3407872 | tf_op jit(solution)/shard_map/dot_general | solution.py:30
  23.1 40.5 %all-reduce.1 = (f32[1536]{0:T(1024)S(1)}, f32[1536]{0:T(1024)S(1)}) all-reduce(f32[1536]{0:T(1024)S(1)} %sub.70, f32[1536]{0:T(1024)S(1)} %add.99), channel_id=1, replica_groups=mesh['grp'=8,'kin'=4] {'grp','kin'}, use_global_device_ids=true, to_apply=%region_0.1 | all-reduce | flops 3072 | bytes 24576 | tf_op jit(solution)/shard_map/psum | solution.py:135
  64.6 0.6 gather_fusion
  65.2 0.6 dynamic-slice
  67.0 2.9 %fusion.4 = f32[256,1536]{1,0:T(8,128)S(1)} fusion(bf16[2,1024,1536]{2,1,0:T(8,128)(2,1)} %param.10, bf16[128,1024]{1,0:T(8,128)(2,1)S(1)} %bitcast.192, bf16[128,1024]{1,0:T(8,128)(2,1)S(1)} %bitcast.190), kind=kOutput, calls=%fused_computation.5 | convolution fusion | flops 806354944 | bytes 5242880 | tf_op jit(solution)/shard_map/dot_general | solution.py:30
  69.9 2.9 %fusion = f32[256,1536]{1,0:T(8,128)S(1)} fusion(bf16[2,1024,1536]{2,1,0:T(8,128)(2,1)} %param.10, bf16[128,1024]{1,0:T(8,128)(2,1)S(1)} %bitcast.193, bf16[128,1024]{1,0:T(8,128)(2,1)S(1)} %bitcast.191), kind=kOutput, calls=%fused_computation.1 | convolution fusion | flops 806354944 | bytes 5242880 | tf_op jit(solution)/shard_map/dot_general | solution.py:31
  73.4 0.4 fusion.20
  74.3 0.4 convolution_subtract_fusion
  74.8 1.0 %fusion.59 = f32[1,4,4,1,1]{2,0,4,1,3:T(1,128)S(1)} fusion(f32[4,4,4,4,4]{4,3,2,1,0:T(4,128)S(1)} %reshape.506, bf16[4,4,4,1,1]{1,3,2,4,0:T(2,128)(2,1)S(1)} %copy.17), kind=kOutput, calls=%fused_computation.118 | convolution fusion | flops 12288 | bytes 4288 | tf_op jit(solution)/shard_map/abcdvw,bwd->avc/dot_general | solution.py:79
  75.7 1.0 %fusion.57 = f32[1,4,4,1,1]{2,0,4,1,3:T(1,128)S(1)} fusion(f32[4,4,4,4,4]{4,3,2,1,0:T(4,128)S(1)} %reshape.506, bf16[4,4,4,1,1]{1,3,2,4,0:T(2,128)(2,1)S(1)} %copy.15), kind=kOutput, calls=%fused_computation.116 | convolution fusion | flops 12288 | bytes 4288 | tf_op jit(solution)/shard_map/abcdvw,bwd->avc/dot_general | solution.py:76
  76.7 1.0 %fusion.60 = f32[1,4,4,1,1]{2,0,4,1,3:T(1,128)S(1)} fusion(f32[4,4,4,4,4]{4,3,2,1,0:T(4,128)S(1)} %reshape.508, bf16[4,4,4,1,1]{1,3,2,4,0:T(2,128)(2,1)S(1)} %copy.15), kind=kOutput, calls=%fused_computation.119 | convolution fusion | flops 12288 | bytes 4288 | tf_op jit(solution)/shard_map/abcdvw,bwd->avc/dot_general | solution.py:79
  77.7 1.0 %fusion.58 = f32[1,4,4,1,1]{2,0,4,1,3:T(1,128)S(1)} fusion(f32[4,4,4,4,4]{4,3,2,1,0:T(4,128)S(1)} %reshape.508, bf16[4,4,4,1,1]{1,3,2,4,0:T(2,128)(2,1)S(1)} %copy.17), kind=kOutput, calls=%fused_computation.117 | convolution fusion | flops 12288 | bytes 4288 | tf_op jit(solution)/shard_map/abcdvw,bwd->avc/dot_general | solution.py:76
  79.7 5.9 %all-reduce = f32[4,2,16]{2,1,0:T(2,128)S(1)} all-reduce(f32[4,2,16]{2,1,0:T(2,128)S(1)} %copy.14), channel_id=2, replica_groups=mesh['grp'=8,'kin'=4] {'kin'}, use_global_device_ids=true, to_apply=%region_2.3.clone | all-reduce | flops 128 | bytes 1024
  85.6 0.6 constant_dynamic-slice_fusion
  86.2 1.6 %collective-permute-start.2 = (f32[1,2,16]{2,1,0:T(2,128)S(1)}, f32[1,2,16]{2,1,0:T(2,128)S(1)}, u32[]{:S(2)}, u32[]{:S(2)}) collective-permute-start(f32[1,2,16]{2,1,0:T(2,128)S(1)} %constant_dynamic-slice_fusion), channel_id=1, source_target_pairs={{0,24},{4,28},{8,0},{12,4},{16,8},{20,12},{24,16},{28,20},{1,25},{... | collective-permute-start | bytes 392 | tf_op jit(solution)/shard_map/ppermute | solution.py:14
  88.2 1.6 %collective-permute-done.2 = f32[1,2,16]{2,1,0:T(2,128)S(1)} collective-permute-done((f32[1,2,16]{2,1,0:T(2,128)S(1)}, f32[1,2,16]{2,1,0:T(2,128)S(1)}, u32[]{:S(2)}, u32[]{:S(2)}) %collective-permute-start.2) | collective-permute-done | bytes 160 | tf_op jit(solution)/shard_map/ppermute | solution.py:14
  89.8 0.6 fusion.41
  (87 shorter events, 5.7 us)
Async XLA Ops:
  0.0 64.6 %copy-start = (f32[32,1536]{1,0:T(8,128)S(1)}, f32[32,1536]{1,0:T(8,128)}, u32[]{:S(2)}) copy-start(f32[32,1536]{1,0:T(8,128)} %param.11) | copy-start | bytes 589828
  6.8 59.3 %collective-permute-start = (bf16[4,2,8,1024]{3,2,1,0:T(8,128)(2,1)S(1)}, bf16[4,2,8,1024]{3,2,1,0:T(8,128)(2,1)S(1)}, u32[]{:S(2)}, u32[]{:S(2)}) collective-permute-start(bf16[4,2,8,1024]{3,2,1,0:T(8,128)(2,1)S(1)} %all_gather.6), channel_id=1, source_target_pairs={{0,8},{4,12},{8,16},{12,20},{16,24},{20,28},{24,0},{28,4},{1,9},{5... | collective-permute-start | bytes 393224 | tf_op jit(solution)/shard_map/ppermute | solution.py:14
  14.5 51.3 %collective-permute-start.1 = (bf16[4,2,16]{2,1,0:T(2,128)(2,1)S(1)}, bf16[4,2,16]{2,1,0:T(2,128)(2,1)S(1)}, u32[]{:S(2)}, u32[]{:S(2)}) collective-permute-start(bf16[4,2,16]{2,1,0:T(2,128)(2,1)S(1)} %all_gather.7), channel_id=1, source_target_pairs={{0,8},{4,12},{8,16},{12,20},{16,24},{20,28},{24,0},{28,4},{1,9},{5... | collective-permute-start | bytes 776 | tf_op jit(solution)/shard_map/ppermute | solution.py:14
  17.1 5.7 %copy-start.4 = (s32[1,32]{1,0:T(1,128)S(1)}, s32[1,32]{1,0:T(1,128)}, u32[]{:S(2)}) copy-start(s32[1,32]{1,0:T(1,128)} %param.13) | copy-start | bytes 388
  17.1 46.4 %copy-start.1 = (f32[1536]{0:T(1024)S(1)}, f32[1536]{0:T(1024)}, u32[]{:S(2)}) copy-start(f32[1536]{0:T(1024)} %param.12) | copy-start | bytes 18436
  19.7 45.5 %copy-start.5 = (u32[32]{0:T(128)S(1)}, u32[32]{0:T(128)}, u32[]{:S(2)}) copy-start(u32[32]{0:T(128)} %constant.55) | copy-start | bytes 388
  72.8 17.1 %copy-start.2 = (f32[1,2,16]{2,1,0:T(2,128)S(1)}, f32[1,2,16]{2,1,0:T(2,128)}, u32[]{:S(2)}) copy-start(f32[1,2,16]{2,1,0:T(2,128)} %param.8) | copy-start | bytes 388
  72.8 17.1 %copy-start.3 = (f32[1,16]{1,0:T(1,128)S(1)}, f32[1,16]{1,0:T(1,128)}, u32[]{:S(2)}) copy-start(f32[1,16]{1,0:T(1,128)} %param.9) | copy-start | bytes 196
  86.2 3.6 %collective-permute-start.2 = (f32[1,2,16]{2,1,0:T(2,128)S(1)}, f32[1,2,16]{2,1,0:T(2,128)S(1)}, u32[]{:S(2)}, u32[]{:S(2)}) collective-permute-start(f32[1,2,16]{2,1,0:T(2,128)S(1)} %constant_dynamic-slice_fusion), channel_id=1, source_target_pairs={{0,24},{4,28},{8,0},{12,4},{16,8},{20,12},{24,16},{28,20},{1,25},{... | collective-permute-start | bytes 392 | tf_op jit(solution)/shard_map/ppermute | solution.py:14
where the time goes:
time: 90.9 us; the launch traced here: 90.4 us
  blocking collectives  58.2 us (64%)
  matrix products  17.3 us (19%)
  starting transfers between devices  5.12 us (6%)
  local copies, waits for them, and re-layouts  4.49 us (5%)
  other arithmetic  3.19 us (4%)
  waiting for transfers between devices  1.65 us (2%)
    psum x1, blocking collectives, on_device(): sum_re, sum_im = lax.psum((part_re, part_im), ('grp', 'kin'))  40.5 us
    all_gather x1, blocking collectives, on_device(): lax.all_gather(waves, 'kin', axis=0, tiled=True)  6.84 us
    unnamed x1, blocking collectives  5.9 us
    dot_general x2, matrix products, densities(): first = jnp.dot(stacked, basis[0], preferred_element_type=jnp.float32)  5.41 us
    dot_general x2, matrix products, densities(): second = jnp.dot(stacked, basis[1], preferred_element_type=jnp.float32)  5.39 us
    ppermute x3, starting transfers between devices, shifted(): return lax.ppermute(value, axis, pairs)  5.12 us
    all_gather x1, blocking collectives, on_device(): lax.all_gather(coarse, 'kin', axis=0, tiled=True)  5.03 us
  transfers between devices with their start and end apart: 3, of which 1 were waited for; matrix products, arithmetic and copies ran while one was open for 12% of the time, Pallas kernels for 0%

commit v1 on v0

v1 whole, which is shorter than its diff:
```python
import functools

import jax
import jax.numpy as jnp
from jax import lax
from jax.experimental import pallas as pl
from jax.experimental.pallas import tpu as pltpu
from jax.sharding import PartitionSpec as P

NV = 4
NC = 4
NB = 8
NT = 16
BLK = 4
ROWS = BLK * NC * NC
CHUNK = 256
MESH = pl.DeviceIdType.MESH
F32 = jnp.float32
BF16 = jnp.bfloat16


def iota(shape, dim):
    return lax.broadcasted_iota(jnp.int32, shape, dim)


def mm(left, right):
    return jnp.dot(left, right, preferred_element_type=F32)


def mm_nt(left, right):
    return lax.dot_general(left, right, (((1,), (1,)), ((), ())), preferred_element_type=F32)


def hi_lo(value):
    high = value.astype(BF16)
    low = (value - high.astype(F32)).astype(BF16)
    return jnp.concatenate([high, low], 0)


def one_hot(cond):
    return jnp.where(cond, 1.0, 0.0).astype(BF16)


def conj_mul(lre, lim, rre, rim):
    return lre * rre + lim * rim, lre * rim - lim * rre


def kernel(
    groups, members, n_k, n_g,
    waves, vector, energies, basis, screening, coulomb, qmap, out,
    basis_v, screen_v, wrecv, vrecv, own_p, pair_p, own_d, s_own, s_a, s_plane, s_b, h_send, h_recv,
    basis_sem, screen_sem, w_ssem, w_rsem, v_ssem, v_rsem, a_ssem, a_rsem, b_ssem, b_rsem, h_ssem, h_rsem,
):
    offset = groups // 4
    planes = 4
    block = members
    points = waves.shape[3]
    n_chunk = n_g // CHUNK
    grp = lax.axis_index("grp")
    kin = lax.axis_index("kin")
    plane = lax.div(grp, offset)
    spot = lax.rem(grp, offset)

    def at(dp, ds, dk):
        g = lax.rem(plane + dp, planes) * offset + lax.rem(spot + ds, offset)
        return (g, lax.rem(kin + dk, members))

    basis_in = []
    for n in range(n_chunk):
        cols = pl.ds(n * CHUNK, CHUNK)
        copy = pltpu.make_async_copy(basis.at[:, :, cols], basis_v.at[:, :, cols], basis_sem.at[n])
        copy.start()
        basis_in.append(copy)
    screen_in = pltpu.make_async_copy(screening, screen_v, screen_sem)
    screen_in.start()

    mates = [(0, ds, dk) for ds in range(offset) for dk in range(members) if (ds, dk) != (0, 0)]
    others = [(dp, 0, dk) for dp in (1, 3) for dk in range(members)] + [(2, 0, 0)]
    barrier = pltpu.get_barrier_semaphore()
    for where in others + mates:
        pl.semaphore_signal(barrier, inc=1, device_id=at(*where), device_id_type=MESH)
    pl.semaphore_wait(barrier, len(others) + len(mates))

    def remote(src, dst, ssem, rsem, where):
        return pltpu.make_async_remote_copy(
            src_ref=src, dst_ref=dst, send_sem=ssem, recv_sem=rsem, device_id=at(*where), device_id_type=MESH
        )

    w_copies = []
    for i in range(members):
        w_copies.append(remote(waves, wrecv.at[pl.ds(i, 1)], w_ssem.at[i], w_rsem.at[i], (1, 0, i)))
        w_copies[-1].start()
    v_copies = []
    for i in range(members):
        v_copies.append(remote(vector, vrecv.at[pl.ds(i, 1)], v_ssem.at[i], v_rsem.at[i], (1, 0, i)))
        v_copies[-1].start()

    low_half = iota((8, points), 0) < 4
    own_re = waves[0, 0].astype(F32)
    own_im = waves[0, 1].astype(F32)

    def cond_twice(part):
        return jnp.concatenate([part[NV:], part[NV:]], 0)

    cre, cim = cond_twice(own_re), cond_twice(own_im)
    re_parts, im_parts = [], []
    for j in range(2):
        vre = jnp.where(low_half, own_re[2 * j:2 * j + 1], own_re[2 * j + 1:2 * j + 2])
        vim = jnp.where(low_half, own_im[2 * j:2 * j + 1], own_im[2 * j + 1:2 * j + 2])
        pre, pim = conj_mul(vre, vim, cre, cim)
        re_parts.append(pre)
        im_parts.append(pim)
    pre = jnp.concatenate(re_parts, 0)
    pim = jnp.concatenate(im_parts, 0)
    own_p[0:NT, 0:points] = pre.astype(BF16)
    own_p[0:NT, points:] = (-pim).astype(BF16)
    own_p[NT:2 * NT, 0:points] = pim.astype(BF16)
    own_p[NT:2 * NT, points:] = pre.astype(BF16)

    own_vec = vector[0]
    x_own = own_vec.astype(BF16).astype(F32)
    xr, xi = x_own[0:1], x_own[1:2]
    x_rows = jnp.concatenate(
        [jnp.concatenate([xr, -xi], 1), jnp.concatenate([xi, xr], 1), jnp.zeros((6, 2 * NT), F32)], 0
    ).astype(BF16)

    def basis_cols(n):
        cols = pl.ds(n * CHUNK, CHUNK)
        return jnp.concatenate([basis_v[0, :, cols], basis_v[1, :, cols]], 0)

    for n in range(n_chunk):
        basis_in[n].wait()
        cols = pl.ds(n * CHUNK, CHUNK)
        dens = mm(own_p[...], basis_cols(n)).astype(BF16)
        own_d[:, cols] = dens
        s_own[:, cols] = mm(x_rows, dens)[0:2]

    a_copies = []
    for i, where in enumerate(mates):
        a_copies.append(remote(s_own, s_a.at[i], a_ssem.at[i], a_rsem.at[i], where))
        a_copies[-1].start()

    side = 2 * ROWS
    row = iota((side, NT), 0)
    lane = iota((side, NT), 1)
    row_b = (row // 32) % 2 * 2 + (row // 4) % 2
    a_band = (row // 8) % 4
    b_band = row % 4
    col = iota((NT, side), 1)
    tr = iota((NT, side), 0)
    pick_v = one_hot((col // 8) % 4 == tr // 4)
    pick_w = one_hot(col % 4 == tr // 4)
    full_r = iota((side, side), 0)
    full_c = iota((side, side), 1)
    same_b = ((full_r // 32) % 2 == (full_c // 32) % 2) & ((full_r // 4) % 2 == (full_c // 4) % 2)
    r_im = full_r >= ROWS
    c_im = full_c >= ROWS
    same_comp = r_im == c_im
    sign = jnp.where(r_im, 1.0, -1.0)

    def spread(x_re, x_im, pick):
        xx_re = jnp.where(same_b, mm(x_re.astype(BF16), pick), 0.0)
        xx_im = jnp.where(same_b, mm(x_im.astype(BF16), pick), 0.0)
        return xx_re, xx_im

    own_rows_re = jnp.where(a_band == lane % 4, xr, 0.0)
    own_rows_im = jnp.where(a_band == lane % 4, xi, 0.0)
    oa_re, oa_im = spread(own_rows_re, own_rows_im, pick_v)
    h_re_w = jnp.where(same_comp, oa_re, -sign * oa_im)
    h_im_w = jnp.where(same_comp, oa_im, sign * oa_re)

    screen_in.wait()
    low_chunk = iota((8, CHUNK), 0) < 4
    base = lax.rem(grp + groups - offset, groups) * block
    s_done = False
    d_re = jnp.zeros((NC * 8, side), F32)
    d_im = jnp.zeros((NC * 8, side), F32)
    q_cat = jnp.concatenate([pick_v, pick_w], 0)
    h_copies = []
    for blk in range(members // BLK):
        slots = [blk * BLK + j for j in range(BLK)]
        for i in slots:
            w_copies[i].wait_recv()
            v_copies[i].wait_recv()

        for kind, first_band in ((0, NV), (1, 0)):
            for q in range(2):
                s0, s1 = slots[2 * q], slots[2 * q + 1]
                rre = jnp.concatenate(
                    [wrecv[s0, 0].astype(F32)[first_band:first_band + 4], wrecv[s1, 0].astype(F32)[first_band:first_band + 4]], 0)
                rim = jnp.concatenate(
                    [wrecv[s0, 1].astype(F32)[first_band:first_band + 4], wrecv[s1, 1].astype(F32)[first_band:first_band + 4]], 0)
                for half in range(2):
                    res, ims = [], []
                    for c in (2 * half, 2 * half + 1):
                        band = first_band + c
                        a, b = conj_mul(own_re[band:band + 1], own_im[band:band + 1], rre, rim)
                        res.append(a)
                        ims.append(b)
                    pre = jnp.concatenate(res, 0)
                    pim = jnp.concatenate(ims, 0)
                    r0 = kind * 2 * ROWS + q * 32 + half * 16
                    pair_p[r0:r0 + 16, 0:points] = pre.astype(BF16)
                    pair_p[r0:r0 + 16, points:] = (-pim).astype(BF16)
                    pair_p[r0 + ROWS:r0 + ROWS + 16, 0:points] = pim.astype(BF16)
                    pair_p[r0 + ROWS:r0 + ROWS + 16, points:] = pre.astype(BF16)

        rows_w = [qmap[0, base + lax.rem(kin + members - i, members)] for i in slots]
        kern = jnp.zeros((side, side), F32)
        for n in range(n_chunk):
            cols = pl.ds(n * CHUNK, CHUNK)
            dens = mm(pair_p[...], basis_cols(n)).astype(BF16)
            tiles = []
            for q in range(2):
                w0 = screen_v[pl.ds(rows_w[2 * q], 1), cols]
                w1 = screen_v[pl.ds(rows_w[2 * q + 1], 1), cols]
                tiles += [jnp.where(low_chunk, w0, w1)] * 4
            weight = jnp.concatenate(tiles * 2, 0)
            cond = (dens[0:side].astype(F32) * weight).astype(BF16)
            kern = kern + mm_nt(cond, dens[side:])
            if n == n_chunk // 2 and not s_done:
                s_done = True
                for copy in a_copies:
                    copy.wait_recv()
                total = s_own[...]
                for i in range(len(mates)):
                    total = total + s_a[i]
                s_plane[...] = total
                b_copies = []
                for i in range(planes - 1):
                    b_copies.append(remote(s_plane, s_b.at[i], b_ssem.at[i], b_rsem.at[i], (i + 1, 0, 0)))
                    b_copies[-1].start()

        part_re = jnp.zeros((side, NT), F32)
        part_im = jnp.zeros((side, NT), F32)
        for j, i in enumerate(slots):
            xb = vrecv[i].astype(BF16).astype(F32)
            hit = (row_b == j) & (b_band == lane % 4)
            part_re = part_re + jnp.where(hit, xb[0:1], 0.0)
            part_im = part_im + jnp.where(hit, xb[1:2], 0.0)
        pa_re, pa_im = spread(part_re, part_im, pick_w)
        d_re_w = jnp.where(same_comp, pa_re, sign * pa_im)
        d_im_w = jnp.where(same_comp, pa_im, -sign * pa_re)

        def fold_d(value):
            return value[0:32] + value[32:64] + value[64:96] + value[96:128]

        def fold_h(value):
            halves = value[0:64] + value[64:128]
            return jnp.concatenate(
                [halves[32 * q:32 * q + 8] + halves[32 * q + 8:32 * q + 16]
                 + halves[32 * q + 16:32 * q + 24] + halves[32 * q + 24:32 * q + 32] for q in range(2)], 0)

        d_re = d_re + fold_d(kern * d_re_w)
        d_im = d_im + fold_d(kern * d_im_w)
        h_rows = jnp.concatenate([fold_h(kern * h_re_w), fold_h(kern * h_im_w)], 0)
        h_sums = mm_nt(hi_lo(h_rows), pick_w)
        h_sums = h_sums[0:32] + h_sums[32:64]
        hr = iota((32, NT), 0)
        hl = iota((32, NT), 1)
        h_sums = jnp.where(hr % 4 == hl % 4, h_sums, 0.0)
        for j, i in enumerate(slots):
            for comp in range(2):
                r0 = comp * 16 + j // 2 * 8
                mine = jnp.where((iota((8, NT), 0) // 4) == j % 2, h_sums[r0:r0 + 8], 0.0)
                h_send[i, comp:comp + 1] = jnp.sum(mine, 0, keepdims=True)
        for i in slots:
            h_copies.append(remote(h_send.at[i], h_recv.at[i], h_ssem.at[i], h_rsem.at[i], (3, 0, members - i)))
            h_copies[-1].start()

    d_sums = mm_nt(hi_lo(jnp.concatenate([d_re, d_im], 0)), pick_v)
    d_sums = d_sums[0:64] + d_sums[64:128]
    dr = iota((64, NT), 0)
    dl = iota((64, NT), 1)
    d_sums = jnp.where((dr // 8) % 4 == dl % 4, d_sums, 0.0)
    direct = jnp.concatenate(
        [jnp.sum(d_sums[0:32], 0, keepdims=True), jnp.sum(d_sums[32:64], 0, keepdims=True)], 0)

    total = s_plane[...]
    for i in range(planes - 1):
        b_copies[i].wait_recv()
        total = total + s_b[i]
    pot = coulomb[...] * total
    pot_rows = jnp.concatenate([hi_lo(pot), jnp.zeros((4, n_g), BF16)], 0)
    ex = mm_nt(pot_rows, own_d[...])
    ex = ex[0:2] + ex[2:4]
    ex_re = ex[0:1, 0:NT] + ex[1:2, NT:]
    ex_im = ex[1:2, 0:NT] - ex[0:1, NT:]
    exchange = jnp.concatenate([ex_re, ex_im], 0)

    scale = 1.0 / n_k
    result = energies[...] * own_vec + (2.0 * scale) * exchange - scale * direct
    back = jnp.zeros((2, NT), F32)
    for i in range(members):
        h_copies[i].wait_recv()
        back = back + h_recv[i]
    out[0] = result - scale * back

    for copy in w_copies + v_copies + a_copies + b_copies + h_copies:
        copy.wait_send()


def on_device(waves, vector, energies, basis, screening, coulomb, qmap):
    groups = lax.axis_size("grp")
    members = lax.axis_size("kin")
    offset = groups // 4
    n_mates = offset * members - 1
    points = waves.shape[3]
    n_g = basis.shape[2]
    vmem = pl.BlockSpec(memory_space=pltpu.VMEM)
    smem = pl.BlockSpec(memory_space=pltpu.SMEM)
    hbm = pl.BlockSpec(memory_space=pl.ANY)
    dma = pltpu.SemaphoreType.DMA
    return pl.pallas_call(
        functools.partial(kernel, groups, members, groups * members, n_g),
        out_shape=jax.ShapeDtypeStruct(vector.shape, F32),
        in_specs=[vmem, vmem, vmem, hbm, hbm, vmem, smem],
        out_specs=vmem,
        scratch_shapes=[
            pltpu.VMEM(basis.shape, BF16),
            pltpu.VMEM(screening.shape, F32),
            pltpu.VMEM((members,) + waves.shape[1:], BF16),
            pltpu.VMEM((members, 2, NT), F32),
            pltpu.VMEM((2 * NT, 2 * points), BF16),
            pltpu.VMEM((4 * ROWS, 2 * points), BF16),
            pltpu.VMEM((2 * NT, n_g), BF16),
            pltpu.VMEM((2, n_g), F32),
            pltpu.VMEM((n_mates, 2, n_g), F32),
            pltpu.VMEM((2, n_g), F32),
            pltpu.VMEM((3, 2, n_g), F32),
            pltpu.VMEM((members, 2, NT), F32),
            pltpu.VMEM((members, 2, NT), F32),
            dma((n_g // CHUNK,)),
            dma,
            dma((members,)), dma((members,)),
            dma((members,)), dma((members,)),
            dma((n_mates,)), dma((n_mates,)),
            dma((3,)), dma((3,)),
            dma((members,)), dma((members,)),
        ],
        compiler_params=pltpu.CompilerParams(
            collective_id=0, has_side_effects=True, vmem_limit_bytes=40 * 1024 * 1024
        ),
    )(waves, vector, energies, basis, screening, coulomb.reshape(1, n_g), qmap)


def solution(mesh):
    return jax.shard_map(
        on_device,
        mesh=mesh,
        in_specs=(
            P(("grp", "kin"), None, None, None),
            P(("grp", "kin"), None, None),
            P(("grp", "kin"), None),
            P(),
            P(),
            P(),
            P(("grp", "kin"), None),
        ),
        out_specs=P(("grp", "kin"), None, None),
        check_vma=False,
    )
```

time: 90.9 us -> 28.1 us (0.31)
  blocking collectives: 58.2 us -> 0 us
  Pallas kernels: 0 us -> 20.1 us
  matrix products: 17.3 us -> 0 us
  starting transfers between devices: 5.12 us -> 0 us
  local copies, waits for them, and re-layouts: 4.49 us -> 7.72 us
  other arithmetic: 3.19 us -> 0 us
  waiting for transfers between devices: 1.65 us -> 0 us
    psum x1 -> x0, blocking collectives: 40.5 us -> none  [on_device(): sum_re, sum_im = lax.psum((part_re, part_im), ('grp', 'kin'))]
    pallas_call x0 -> x1, Pallas kernels: none -> 20.1 us  [on_device(): pl.pallas_call(functools.partial(kernel, groups, members, groups * member...]
    dot_general x20 -> x0, matrix products: 17.3 us -> none  [the longest x2 5.41 us: densities(): first = jnp.dot(stacked, basis[0], preferred_element_type=jnp.float32)]
    all_gather x2 -> x0, blocking collectives: 11.9 us -> none  [the longest x1 6.84 us: on_device(): lax.all_gather(waves, 'kin', axis=0, tiled=True)]
    unnamed x1 -> x0, blocking collectives: 5.9 us -> none
    unnamed x16 -> x13, local copies, waits for them, and re-layouts: 1.45 us -> 7.02 us
    ppermute x3 -> x0, starting transfers between devices: 5.12 us -> none  [shifted(): return lax.ppermute(value, axis, pairs)]
    ppermute x3 -> x0, waiting for transfers between devices: 1.65 us -> none  [shifted(): return lax.ppermute(value, axis, pairs)]
  transfers between devices with their start and end apart: 3 -> 0, of which waited for: 1 -> 0; matrix products, arithmetic and copies ran while one was open for 12% -> 0% of each run, Pallas kernels for 0% -> 0%
where the time goes in v1:
time: 28.1 us; the launch traced here: 27.8 us
  Pallas kernels  20.1 us (72%)
  local copies, waits for them, and re-layouts  7.72 us (27%)
    pallas_call x1, Pallas kernels, on_device(): pl.pallas_call(functools.partial(kernel, groups, members, groups * member...  20.1 us
    unnamed x13, local copies, waits for them, and re-layouts  7.02 us
    reshape x1, local copies, waits for them, and re-layouts, on_device(): coulomb.reshape(1, n_g)  0.7 us

profile of v1, /device:TPU:0, one launch (start us, length us, event | category | flops | bytes accessed | tf_op | source)
XLA Modules:
  0.0 27.8 jit_solution(12544967455069449816)
XLA Ops:
  0.0 0.7 %reshape.3.coulomb = f32[1,1536]{1,0:T(1,128)S(1)} reshape(f32[1536]{0:T(1024)} %param.12) | data formatting | bytes 12288 | tf_op jit(solution)/shard_map/reshape | solution.py:344
  0.7 0.0 copy-start
  0.7 2.8 %copy-done = bf16[2,1024,1536]{2,1,0:T(8,128)(2,1)S(1)} copy-done((bf16[2,1024,1536]{2,1,0:T(8,128)(2,1)S(1)}, bf16[2,1024,1536]{2,1,0:T(8,128)(2,1)}, u32[]{:S(2)}) %copy-start) | copy-done | bytes 6291480
  3.5 0.0 copy-start.1
  3.5 0.9 %copy-done.1 = f32[32,1536]{1,0:T(8,128)S(1)} copy-done((f32[32,1536]{1,0:T(8,128)S(1)}, f32[32,1536]{1,0:T(8,128)}, u32[]{:S(2)}) %copy-start.1) | copy-done | bytes 196632
  4.4 0.0 copy-start.2
  4.4 0.8 %copy-done.2 = bf16[1,2,8,1024]{3,2,1,0:T(8,128)(2,1)S(1)} copy-done((bf16[1,2,8,1024]{3,2,1,0:T(8,128)(2,1)S(1)}, bf16[1,2,8,1024]{3,2,1,0:T(8,128)(2,1)}, u32[]{:S(2)}) %copy-start.2) | copy-done | bytes 32792
  5.2 0.0 copy-start.3
  5.2 0.7 %copy-done.3 = f32[1,2,16]{2,1,0:T(2,128)S(1)} copy-done((f32[1,2,16]{2,1,0:T(2,128)S(1)}, f32[1,2,16]{2,1,0:T(2,128)}, u32[]{:S(2)}) %copy-start.3) | copy-done | bytes 152
  5.9 0.0 copy-start.4
  5.9 0.7 %copy-done.4 = f32[1,16]{1,0:T(1,128)S(1)} copy-done((f32[1,16]{1,0:T(1,128)S(1)}, f32[1,16]{1,0:T(1,128)}, u32[]{:S(2)}) %copy-start.4) | copy-done | bytes 88
  6.5 0.0 copy-start.5
  6.5 0.7 %copy-done.5 = s32[1,32]{1,0:T(1,128)S(1)} copy-done((s32[1,32]{1,0:T(1,128)S(1)}, s32[1,32]{1,0:T(1,128)}, u32[]{:S(2)}) %copy-start.5) | copy-done | bytes 152
  7.2 20.1 %shard_map.73 = f32[1,2,16]{2,1,0:T(2,128)S(1)} custom-call(bf16[1,2,8,1024]{3,2,1,0:T(8,128)(2,1)S(1)} %copy-done.2, f32[1,2,16]{2,1,0:T(2,128)S(1)} %copy-done.3, f32[1,16]{1,0:T(1,128)S(1)} %copy-done.4, bf16[2,1024,1536]{2,1,0:T(8,128)(2,1)S(1)} %copy-done, f32[32,1536]{1,0:T(8,128)S(1)} %copy-done.1, f32[1,1536]{1,0:T(1,128)S(1)} %reshape.3.coulomb, ...), custom_call_target="tpu_custom_call" | custom-call | tf_op jit(solution)/shard_map/pallas_call | solution.py:314
  27.2 0.6 %copy.9 = f32[1,2,16]{2,1,0:T(2,128)} copy(f32[1,2,16]{2,1,0:T(2,128)S(1)} %shard_map.73) | data formatting | bytes 256
Async XLA Ops:
  0.7 2.8 %copy-start = (bf16[2,1024,1536]{2,1,0:T(8,128)(2,1)S(1)}, bf16[2,1024,1536]{2,1,0:T(8,128)(2,1)}, u32[]{:S(2)}) copy-start(bf16[2,1024,1536]{2,1,0:T(8,128)(2,1)} %basis.1) | copy-start | bytes 18874372
  3.5 0.9 %copy-start.1 = (f32[32,1536]{1,0:T(8,128)S(1)}, f32[32,1536]{1,0:T(8,128)}, u32[]{:S(2)}) copy-start(f32[32,1536]{1,0:T(8,128)} %screening.1) | copy-start | bytes 589828
  4.4 0.8 %copy-start.2 = (bf16[1,2,8,1024]{3,2,1,0:T(8,128)(2,1)S(1)}, bf16[1,2,8,1024]{3,2,1,0:T(8,128)(2,1)}, u32[]{:S(2)}) copy-start(bf16[1,2,8,1024]{3,2,1,0:T(8,128)(2,1)} %waves.1) | copy-start | bytes 98308
  5.2 0.7 %copy-start.3 = (f32[1,2,16]{2,1,0:T(2,128)S(1)}, f32[1,2,16]{2,1,0:T(2,128)}, u32[]{:S(2)}) copy-start(f32[1,2,16]{2,1,0:T(2,128)} %vector.1) | copy-start | bytes 388
  5.9 0.7 %copy-start.4 = (f32[1,16]{1,0:T(1,128)S(1)}, f32[1,16]{1,0:T(1,128)}, u32[]{:S(2)}) copy-start(f32[1,16]{1,0:T(1,128)} %energies.1) | copy-start | bytes 196
  6.5 0.7 %copy-start.5 = (s32[1,32]{1,0:T(1,128)S(1)}, s32[1,32]{1,0:T(1,128)}, u32[]{:S(2)}) copy-start(s32[1,32]{1,0:T(1,128)} %qmap.1) | copy-start | bytes 388

commit v2 on v1

--- a/solution.py
+++ b/solution.py
@@ -47,14 +47,14 @@
 
 def kernel(
     groups, members, n_k, n_g,
-    waves, vector, energies, basis, screening, coulomb, qmap, out,
-    basis_v, screen_v, wrecv, vrecv, own_p, pair_p, own_d, s_own, s_a, s_plane, s_b, h_send, h_recv,
-    basis_sem, screen_sem, w_ssem, w_rsem, v_ssem, v_rsem, a_ssem, a_rsem, b_ssem, b_rsem, h_ssem, h_rsem,
+    waves_h, vector_h, energies_h, basis, screening, coulomb_h, qmap_h, out,
+    waves, vector, energies, coulomb, qmap, basis_v, screen_v, wrecv, vrecv, own_p, pair_p, own_d, s_own, s_a, s_plane, s_b, h_send, h_recv,
+    small_sem, basis_sem, screen_sem, w_ssem, w_rsem, v_ssem, v_rsem, a_ssem, a_rsem, b_ssem, b_rsem, h_ssem, h_rsem,
 ):
     offset = groups // 4
     planes = 4
     block = members
-    points = waves.shape[3]
+    points = waves_h.shape[3]
     n_chunk = n_g // CHUNK
     grp = lax.axis_index("grp")
     kin = lax.axis_index("kin")
@@ -65,6 +65,11 @@
         g = lax.rem(plane + dp, planes) * offset + lax.rem(spot + ds, offset)
         return (g, lax.rem(kin + dk, members))
 
+    small = []
+    pairs = [(waves_h, waves), (vector_h, vector), (energies_h, energies), (coulomb_h, coulomb), (qmap_h, qmap)]
+    for i, (src, dst) in enumerate(pairs):
+        small.append(pltpu.make_async_copy(src, dst, small_sem.at[i]))
+        small[-1].start()
     basis_in = []
     for n in range(n_chunk):
         cols = pl.ds(n * CHUNK, CHUNK)
@@ -88,13 +93,15 @@
 
     w_copies = []
     for i in range(members):
-        w_copies.append(remote(waves, wrecv.at[pl.ds(i, 1)], w_ssem.at[i], w_rsem.at[i], (1, 0, i)))
+        w_copies.append(remote(waves_h, wrecv.at[pl.ds(i, 1)], w_ssem.at[i], w_rsem.at[i], (1, 0, i)))
         w_copies[-1].start()
     v_copies = []
     for i in range(members):
-        v_copies.append(remote(vector, vrecv.at[pl.ds(i, 1)], v_ssem.at[i], v_rsem.at[i], (1, 0, i)))
+        v_copies.append(remote(vector_h, vrecv.at[pl.ds(i, 1)], v_ssem.at[i], v_rsem.at[i], (1, 0, i)))
         v_copies[-1].start()
 
+    for copy in small:
+        copy.wait()
     low_half = iota((8, points), 0) < 4
     own_re = waves[0, 0].astype(F32)
     own_im = waves[0, 1].astype(F32)
@@ -280,7 +287,7 @@
     for i in range(planes - 1):
         b_copies[i].wait_recv()
         total = total + s_b[i]
-    pot = coulomb[...] * total
+    pot = coulomb[...].reshape(1, n_g) * total
     pot_rows = jnp.concatenate([hi_lo(pot), jnp.zeros((4, n_g), BF16)], 0)
     ex = mm_nt(pot_rows, own_d[...])
     ex = ex[0:2] + ex[2:4]
@@ -308,15 +315,19 @@
     points = waves.shape[3]
     n_g = basis.shape[2]
     vmem = pl.BlockSpec(memory_space=pltpu.VMEM)
-    smem = pl.BlockSpec(memory_space=pltpu.SMEM)
     hbm = pl.BlockSpec(memory_space=pl.ANY)
     dma = pltpu.SemaphoreType.DMA
     return pl.pallas_call(
         functools.partial(kernel, groups, members, groups * members, n_g),
         out_shape=jax.ShapeDtypeStruct(vector.shape, F32),
-        in_specs=[vmem, vmem, vmem, hbm, hbm, vmem, smem],
+        in_specs=[hbm] * 7,
         out_specs=vmem,
         scratch_shapes=[
+            pltpu.VMEM(waves.shape, BF16),
+            pltpu.VMEM(vector.shape, F32),
+            pltpu.VMEM(energies.shape, F32),
+            pltpu.VMEM(coulomb.shape, F32),
+            pltpu.SMEM(qmap.shape, jnp.int32),
             pltpu.VMEM(basis.shape, BF16),
             pltpu.VMEM(screening.shape, F32),
             pltpu.VMEM((members,) + waves.shape[1:], BF16),
@@ -330,6 +341,7 @@
             pltpu.VMEM((3, 2, n_g), F32),
             pltpu.VMEM((members, 2, NT), F32),
             pltpu.VMEM((members, 2, NT), F32),
+            dma((5,)),
             dma((n_g // CHUNK,)),
             dma,
             dma((members,)), dma((members,)),
@@ -339,9 +351,9 @@
             dma((members,)), dma((members,)),
         ],
         compiler_params=pltpu.CompilerParams(
-            collective_id=0, has_side_effects=True, vmem_limit_bytes=40 * 1024 * 1024
+            collective_id=0, has_side_effects=True, vmem_limit_bytes=60 * 1024 * 1024
         ),
-    )(waves, vector, energies, basis, screening, coulomb.reshape(1, n_g), qmap)
+    )(waves, vector, energies, basis, screening, coulomb, qmap)
 
 
 def solution(mesh):

time: 28.1 us -> 21 us (0.75)
  local copies, waits for them, and re-layouts: 7.72 us -> 1.24 us
  Pallas kernels: 20.1 us -> 19.6 us
    unnamed x13 -> x1, local copies, waits for them, and re-layouts: 7.02 us -> 1.24 us
    reshape x1 -> x0, local copies, waits for them, and re-layouts: 0.7 us -> none  [on_device(): coulomb.reshape(1, n_g)]
    pallas_call x1, Pallas kernels: 20.1 us -> 19.6 us  [on_device(): pl.pallas_call(functools.partial(kernel, groups, members, groups * member...]
where the time goes in v2:
time: 21 us; the launch traced here: 20.8 us
  Pallas kernels  19.6 us (93%)
  local copies, waits for them, and re-layouts  1.24 us (6%)
    pallas_call x1, Pallas kernels, on_device(): pl.pallas_call(functools.partial(kernel, groups, members, groups * member...  19.6 us
    unnamed x1, local copies, waits for them, and re-layouts  1.24 us

profile of v2, /device:TPU:0, one launch (start us, length us, event | category | flops | bytes accessed | tf_op | source)
XLA Modules:
  0.0 20.8 jit_solution(9614488691429894156)
XLA Ops:
  0.0 19.6 %shard_map.73 = f32[1,2,16]{2,1,0:T(2,128)} custom-call(bf16[1,2,8,1024]{3,2,1,0:T(8,128)(2,1)} %waves_h.1, f32[1,2,16]{2,1,0:T(2,128)} %vector_h.1, f32[1,16]{1,0:T(1,128)} %energies_h.1, bf16[2,1024,1536]{2,1,0:T(8,128)(2,1)} %basis.1, f32[32,1536]{1,0:T(8,128)} %screening.1, f32[1536]{0:T(1024)} %coulomb_h.1, s32[1,32]{1,0:T(1,128)} %qmap_h.1), custom_call_target="tpu_custom_call" | custom-call | tf_op jit(solution)/shard_map/pallas_call | solution.py:320
  19.6 1.2 %copy.9 = f32[1,2,16]{2,1,0:T(2,128)} copy(f32[1,2,16]{2,1,0:T(2,128)} %shard_map.73) | data formatting | bytes 256

commit v3 on v0

v3 whole, which is shorter than its diff:
```python
import functools

import jax
import jax.numpy as jnp
from jax import lax
from jax.experimental import pallas as pl
from jax.experimental.pallas import tpu as pltpu
from jax.sharding import PartitionSpec as P

NV = 4
NC = 4
NT = 16
TEAM = 4
ROWS = TEAM * NT
MESH = pl.DeviceIdType.MESH
F32 = jnp.float32
BF16 = jnp.bfloat16


def iota(shape, dim):
    return lax.broadcasted_iota(jnp.int32, shape, dim)


def mm(left, right):
    return jnp.dot(left, right, preferred_element_type=F32)


def mm_nt(left, right):
    return lax.dot_general(left, right, (((1,), (1,)), ((), ())), preferred_element_type=F32)


def hi_lo(value):
    high = value.astype(BF16)
    low = (value - high.astype(F32)).astype(BF16)
    return jnp.concatenate([high, low], 0)


def one_hot(cond):
    return jnp.where(cond, 1.0, 0.0).astype(BF16)


def conj_mul(lre, lim, rre, rim):
    return lre * rre + lim * rim, lre * rim - lim * rre


def twice(rows):
    return jnp.concatenate([rows, rows], 0)


def kernel(
    groups, members, n_g,
    waves_h, vector_h, energies_h, basis_h, screening_h, coulomb_h, qmap_h, out,
    vector, energies, coulomb, qmap, basis, screening,
    stage, team, part, left, weights, weights_in, own_p, pair_p, own_d, s_own, s_in, h_send, h_recv, t_send, t_recv,
    small_sem, basis_sem, screen_sem, t_ssem, t_rsem, p_ssem, p_rsem, r_ssem, r_rsem,
    w_ssem, w_rsem, s_ssem, s_rsem, h_ssem, h_rsem, d_ssem, d_rsem,
):
    offset = groups // 4
    half = members // 2
    teams = members // TEAM
    n_k = groups * members
    points = waves_h.shape[3]
    quarter = n_g // TEAM
    grp = lax.axis_index("grp")
    kin = lax.axis_index("kin")
    rank = lax.rem(kin, TEAM)
    sib = kin + 1 - 2 * lax.rem(kin, 2)

    def mate(s, who=kin):
        who = who + (s % 2) * (1 - 2 * lax.rem(who, 2))
        return who + (s // 2) * (2 - 4 * lax.rem(lax.div(who, 2), 2))

    def source(i):
        if i < half:
            return lax.rem(kin + members - 2 * i, members)
        return lax.rem(sib + members - 2 * (i - half), members)

    up = lax.rem(grp + offset, groups)
    down = lax.rem(grp + groups - offset, groups)

    my_cols = pl.ds(pl.multiple_of(rank * quarter, 128), quarter)
    pairs = [
        (waves_h.at[0], stage.at[:, :, 0:points]), (vector_h, vector), (qmap_h, qmap),
        (energies_h, energies), (coulomb_h, coulomb),
    ]
    small = []
    for i, (src, dst) in enumerate(pairs):
        small.append(pltpu.make_async_copy(src, dst, small_sem.at[i]))
        small[-1].start()
    screen_in = pltpu.make_async_copy(screening_h, screening, screen_sem)
    screen_in.start()
    basis_in = pltpu.make_async_copy(basis_h.at[:, :, my_cols], basis, basis_sem)
    basis_in.start()

    rel_s = [(dg, dt) for dg in range(groups) for dt in range(teams) if (dg, dt) != (0, 0)]

    def s_target(dg, dt):
        return (lax.rem(grp + dg, groups), lax.rem(kin + dt * TEAM, members))

    barrier = pltpu.get_barrier_semaphore()
    greet = [s_target(dg, dt) for dg, dt in rel_s] + [(grp, mate(s)) for s in range(1, TEAM)]
    for dk in range(members):
        if dk % TEAM:
            greet += [(up, lax.rem(kin + dk, members)), (down, lax.rem(kin + dk, members))]
    for target in greet:
        pl.semaphore_signal(barrier, inc=1, device_id=target, device_id_type=MESH)

    for copy in small:
        copy.wait()
    own_vec = vector[0]
    x_pad = jnp.concatenate([own_vec, jnp.zeros((2, 128 - NT), F32)], 1)
    for comp in range(2):
        stage[comp, :, points:] = jnp.broadcast_to(x_pad[comp:comp + 1], (8, 128)).astype(BF16)
    pl.semaphore_wait(barrier, len(greet))

    def remote(src, dst, ssem, rsem, target):
        return pltpu.make_async_remote_copy(
            src_ref=src, dst_ref=dst, send_sem=ssem, recv_sem=rsem, device_id=target, device_id_type=MESH
        )

    started = []

    def go(copy):
        copy.start()
        started.append(copy)
        return copy

    team_in = [None] * TEAM
    for s in (2, 1):
        team_in[s] = go(remote(stage, team.at[s], t_ssem.at[s], t_rsem.at[s], (grp, mate(s))))
    part_in = [None] * members
    for i in range(half):
        part_in[i] = go(remote(stage, part.at[i], p_ssem.at[i], p_rsem.at[i], (up, lax.rem(kin + 2 * i, members))))

    screen_in.wait()
    base = down * members
    for b in range(members):
        weights[b:b + 1, :] = screening[pl.ds(qmap[0, base + b], 1), :]
    weight_in = [None] * TEAM
    for s in range(1, TEAM):
        cols = pl.ds(pl.multiple_of(lax.rem(mate(s), TEAM) * quarter, 128), quarter)
        weight_in[s] = go(remote(weights.at[:, cols], weights_in.at[s], w_ssem.at[s], w_rsem.at[s], (grp, mate(s))))
    weights_in[0] = weights[:, my_cols]

    side = 2 * ROWS
    col = iota((NT, side), 1)
    tr = iota((NT, side), 0)
    pick_v = one_hot((col // 4) % 4 == tr // 4)
    pick_w = one_hot(col % 4 == tr // 4)
    same_a = (iota((side, side), 0) // NT) % TEAM == (iota((side, side), 1) // NT) % TEAM
    first = iota((8, side), 1) < ROWS
    low_half = iota((8, points), 0) < 4
    row8 = iota((8, NT), 0)
    lane8 = iota((8, NT), 1)

    xs = []
    team_in[3] = remote(team.at[2], team.at[3], t_ssem.at[3], t_rsem.at[3], (grp, sib))
    for s in range(TEAM):
        if s == 1:
            team_in[2].wait_recv()
            go(team_in[3])
        if s in (1, 3):
            team_in[s].wait_recv()
        src = stage if s == 0 else team.at[s]
        wre = src[0, :, 0:points].astype(F32)
        wim = src[1, :, 0:points].astype(F32)
        xs.append((src[0, :, points:].astype(F32)[0:1, 0:NT], src[1, :, points:].astype(F32)[0:1, 0:NT]))
        cre, cim = twice(wre[NV:]), twice(wim[NV:])
        res, ims = [], []
        for h in range(4):
            lre = jnp.where(low_half, wre[2 * h:2 * h + 1], wre[2 * h + 1:2 * h + 2])
            lim = jnp.where(low_half, wim[2 * h:2 * h + 1], wim[2 * h + 1:2 * h + 2])
            left[s, h, 0] = lre
            left[s, h, 1] = lim
            if h < 2:
                pre, pim = conj_mul(lre, lim, cre, cim)
                res.append(pre)
                ims.append(pim)
        pre = jnp.concatenate(res, 0)
        pim = jnp.concatenate(ims, 0)
        r0 = s * NT
        own_p[r0:r0 + NT, 0:points] = pre.astype(BF16)
        own_p[r0:r0 + NT, points:] = (-pim).astype(BF16)
        own_p[ROWS + r0:ROWS + r0 + NT, 0:points] = pim.astype(BF16)
        own_p[ROWS + r0:ROWS + r0 + NT, points:] = pre.astype(BF16)

    xr = jnp.concatenate([x[0] for x in xs], 1)
    xi = jnp.concatenate([x[1] for x in xs], 1)
    x_rows = jnp.concatenate(
        [jnp.concatenate([xr, -xi], 1), jnp.concatenate([xi, xr], 1), jnp.zeros((6, side), F32)], 0
    ).astype(BF16)

    basis_in.wait()
    dens = mm(own_p[...], basis[...].reshape(2 * points, quarter)).astype(BF16)
    own_d[...] = dens
    s_own[...] = mm(x_rows, dens)[0:2]
    s_copies = []
    for i, (dg, dt) in enumerate(rel_s):
        s_copies.append(go(remote(s_own, s_in.at[i], s_ssem.at[i], s_rsem.at[i], s_target(dg, dt))))

    a_re, a_im = [], []
    for s in range(TEAM):
        for c in range(0, NC, 2):
            hit = lane8 % 4 == c + row8 // 4
            a_re.append(jnp.where(hit, xs[s][0], 0.0))
            a_im.append(jnp.where(hit, xs[s][1], 0.0))
    spread = mm(jnp.concatenate(a_re + a_im, 0).astype(BF16), pick_v)
    a_re, a_im = spread[0:ROWS], spread[ROWS:]
    first_all = iota((ROWS, side), 1) < ROWS
    u1 = jnp.where(first_all, a_re, a_im)
    u2 = jnp.where(first_all, -a_im, a_re)

    for s in range(1, TEAM):
        weight_in[s].wait_recv()

    d_re = jnp.zeros((ROWS, side), F32)
    d_im = jnp.zeros((ROWS, side), F32)
    exchange = None
    h_copies = []
    for i in range(members):
        if i >= half:
            part_in[i] = remote(part.at[i - half], part.at[i], r_ssem.at[i - half], r_rsem.at[i - half], (grp, sib))
        part_in[i].wait_recv()
        if i < half:
            go(remote(part.at[i], part.at[half + i], r_ssem.at[i], r_rsem.at[i], (grp, sib)))
        if i == members - 1:
            total = s_own[...]
            for j, copy in enumerate(s_copies):
                copy.wait_recv()
                total = total + s_in[j]
            pot = coulomb[my_cols].reshape(1, quarter) * total
            ex = mm_nt(jnp.concatenate([hi_lo(pot), jnp.zeros((4, quarter), BF16)], 0), own_d[...])
            ex = ex[0:2] + ex[2:4]
            exchange = jnp.concatenate(
                [ex[0:1, 0:ROWS] + ex[1:2, ROWS:], ex[1:2, 0:ROWS] - ex[0:1, ROWS:]], 0)

        slot = i % 2
        wre = part[i, 0, :, 0:points].astype(F32)
        wim = part[i, 1, :, 0:points].astype(F32)
        for kind in range(2):
            rows = slice(NV, NV + NC) if kind == 0 else slice(0, NV)
            rre, rim = twice(wre[rows]), twice(wim[rows])
            for s in range(TEAM):
                res, ims = [], []
                for h in range(2):
                    t = h + 2 - 2 * kind
                    pre, pim = conj_mul(left[s, t, 0], left[s, t, 1], rre, rim)
                    res.append(pre)
                    ims.append(pim)
                pre = jnp.concatenate(res, 0)
                pim = jnp.concatenate(ims, 0)
                r0 = kind * side + s * NT
                pair_p[slot, r0:r0 + NT, 0:points] = pre.astype(BF16)
                pair_p[slot, r0:r0 + NT, points:] = (-pim).astype(BF16)
                pair_p[slot, ROWS + r0:ROWS + r0 + NT, 0:points] = pim.astype(BF16)
                pair_p[slot, ROWS + r0:ROWS + r0 + NT, points:] = pre.astype(BF16)

        dens = mm(pair_p[slot], basis[...].reshape(2 * points, quarter)).astype(BF16)
        b = source(i)
        weight = jnp.concatenate(
            [jnp.broadcast_to(weights_in[s, pl.ds(b, 1), :], (NT, quarter)) for s in range(TEAM)] * 2, 0)
        cond = (dens[0:side].astype(F32) * weight).astype(BF16)
        kern = jnp.where(same_a, mm_nt(cond, dens[side:]), 0.0)
        k_re, k_im = kern[0:ROWS], kern[ROWS:]

        h_re = k_re * u1 + k_im * u2
        h_im = k_im * u1 - k_re * u2

        def fold(value):
            total = value[0:8]
            for r in range(8, ROWS, 8):
                total = total + value[r:r + 8]
            return total

        h_sums = mm_nt(hi_lo(jnp.concatenate([fold(h_re), fold(h_im)], 0)), pick_w)
        h_sums = h_sums[0:16] + h_sums[16:32]
        hit = row8 % 4 == lane8 % 4
        h_send[i] = jnp.concatenate(
            [jnp.sum(jnp.where(hit, h_sums[0:8], 0.0), 0, keepdims=True),
             jnp.sum(jnp.where(hit, h_sums[8:16], 0.0), 0, keepdims=True)], 0)
        h_copies.append(go(remote(h_send.at[i], h_recv.at[i], h_ssem.at[i], h_rsem.at[i], (down, b))))

        xbr = part[i, 0, :, points:].astype(F32)[:, 0:NT]
        xbi = part[i, 1, :, points:].astype(F32)[:, 0:NT]
        xx = mm(jnp.concatenate([jnp.where(hit, xbr, 0.0), jnp.where(hit, xbi, 0.0)], 0).astype(BF16), pick_w)
        w1 = jnp.where(first, xx[0:8], -xx[8:16])
        w2 = jnp.where(first, xx[8:16], xx[0:8])
        w1 = jnp.concatenate([w1] * (ROWS // 8), 0)
        w2 = jnp.concatenate([w2] * (ROWS // 8), 0)
        d_re = d_re + (k_re * w1 + k_im * w2)
        d_im = d_im + (k_re * w2 - k_im * w1)

    scale = 1.0 / n_k
    d_sums = mm_nt(hi_lo(jnp.concatenate([d_re, d_im], 0)), pick_v)
    d_sums = d_sums[0:side] + d_sums[side:]
    d_sums = jnp.where((iota((side, NT), 0) // 4) % 4 == iota((side, NT), 1) % 4, d_sums, 0.0)
    mine = None
    d_copies = []
    for s in (3, 2, 1, 0):
        direct = jnp.concatenate(
            [jnp.sum(d_sums[r:r + NT], 0, keepdims=True) for r in (s * NT, ROWS + s * NT)], 0)
        both = (2.0 * scale) * exchange[:, s * NT:(s + 1) * NT] - scale * direct
        if s == 0:
            mine = both
        else:
            t_send[s] = both
            d_copies.append(go(remote(t_send.at[s], t_recv.at[s], d_ssem.at[s], d_rsem.at[s], (grp, mate(s)))))

    result = energies[...] * own_vec + mine
    for copy in h_copies:
        copy.wait_recv()
    back = h_recv[0]
    for i in range(1, members):
        back = back + h_recv[i]
    for copy in d_copies:
        copy.wait_recv()
    for s in range(1, TEAM):
        result = result + t_recv[s]
    out[0] = result - scale * back

    for copy in started:
        copy.wait_send()


def on_device(waves, vector, energies, basis, screening, coulomb, qmap):
    groups = lax.axis_size("grp")
    members = lax.axis_size("kin")
    half = members // 2
    n_s = groups * (members // TEAM) - 1
    points = waves.shape[3]
    n_g = basis.shape[2]
    quarter = n_g // TEAM
    any_space = pl.BlockSpec(memory_space=pl.ANY)
    dma = pltpu.SemaphoreType.DMA
    vmem = pltpu.VMEM
    stage = (2, 8, points + 128)
    return pl.pallas_call(
        functools.partial(kernel, groups, members, n_g),
        out_shape=jax.ShapeDtypeStruct(vector.shape, F32),
        in_specs=[any_space] * 7,
        out_specs=pl.BlockSpec(memory_space=vmem),
        scratch_shapes=[
            vmem(vector.shape, F32),
            vmem(energies.shape, F32),
            vmem(coulomb.shape, F32),
            pltpu.SMEM(qmap.shape, jnp.int32),
            vmem((2, points, quarter), BF16),
            vmem(screening.shape, F32),
            vmem(stage, BF16),
            vmem((TEAM,) + stage, BF16),
            vmem((members,) + stage, BF16),
            vmem((TEAM, 4, 2, 8, points), F32),
            vmem((members, n_g), F32),
            vmem((TEAM, members, quarter), F32),
            vmem((2 * ROWS, 2 * points), BF16),
            vmem((2, 4 * ROWS, 2 * points), BF16),
            vmem((2 * ROWS, quarter), BF16),
            vmem((2, quarter), F32),
            vmem((n_s, 2, quarter), F32),
            vmem((members, 2, NT), F32),
            vmem((members, 2, NT), F32),
            vmem((TEAM, 2, NT), F32),
            vmem((TEAM, 2, NT), F32),
            dma((5,)), dma, dma,
            dma((TEAM,)), dma((TEAM,)),
            dma((half,)), dma((half,)),
            dma((half,)), dma((half,)),
            dma((TEAM,)), dma((TEAM,)),
            dma((n_s,)), dma((n_s,)),
            dma((members,)), dma((members,)),
            dma((TEAM,)), dma((TEAM,)),
        ],
        compiler_params=pltpu.CompilerParams(
            collective_id=0, has_side_effects=True, vmem_limit_bytes=60 * 1024 * 1024
        ),
    )(waves, vector, energies, basis, screening, coulomb, qmap)


def solution(mesh):
    return jax.shard_map(
        on_device,
        mesh=mesh,
        in_specs=(
            P(("grp", "kin"), None, None, None),
            P(("grp", "kin"), None, None),
            P(("grp", "kin"), None),
            P(),
            P(),
            P(),
            P(("grp", "kin"), None),
        ),
        out_specs=P(("grp", "kin"), None, None),
        check_vma=False,
    )
```

time: 90.9 us -> 21.1 us (0.23)
  blocking collectives: 58.2 us -> 0 us
  Pallas kernels: 0 us -> 19.7 us
  matrix products: 17.3 us -> 0 us
  starting transfers between devices: 5.12 us -> 0 us
  local copies, waits for them, and re-layouts: 4.49 us -> 1.24 us
  other arithmetic: 3.19 us -> 0 us
  waiting for transfers between devices: 1.65 us -> 0 us
    psum x1 -> x0, blocking collectives: 40.5 us -> none  [on_device(): sum_re, sum_im = lax.psum((part_re, part_im), ('grp', 'kin'))]
    pallas_call x0 -> x1, Pallas kernels: none -> 19.7 us  [on_device(): pl.pallas_call(functools.partial(kernel, groups, members, n_g), out_shape...]
    dot_general x20 -> x0, matrix products: 17.3 us -> none  [the longest x2 5.41 us: densities(): first = jnp.dot(stacked, basis[0], preferred_element_type=jnp.float32)]
    all_gather x2 -> x0, blocking collectives: 11.9 us -> none  [the longest x1 6.84 us: on_device(): lax.all_gather(waves, 'kin', axis=0, tiled=True)]
    unnamed x1 -> x0, blocking collectives: 5.9 us -> none
    ppermute x3 -> x0, starting transfers between devices: 5.12 us -> none  [shifted(): return lax.ppermute(value, axis, pairs)]
    ppermute x3 -> x0, waiting for transfers between devices: 1.65 us -> none  [shifted(): return lax.ppermute(value, axis, pairs)]
    convert_element_type x7 -> x0, other arithmetic: 1.2 us -> none  [the longest x1 0.68 us: on_device(): coarse = vector.astype(jnp.bfloat16)]
  transfers between devices with their start and end apart: 3 -> 0, of which waited for: 1 -> 0; matrix products, arithmetic and copies ran while one was open for 12% -> 0% of each run, Pallas kernels for 0% -> 0%
where the time goes in v3:
time: 21.1 us; the launch traced here: 20.9 us
  Pallas kernels  19.7 us (93%)
  local copies, waits for them, and re-layouts  1.24 us (6%)
    pallas_call x1, Pallas kernels, on_device(): pl.pallas_call(functools.partial(kernel, groups, members, n_g), out_shape...  19.7 us
    unnamed x1, local copies, waits for them, and re-layouts  1.24 us

profile of v3, /device:TPU:0, one launch (start us, length us, event | category | flops | bytes accessed | tf_op | source)
XLA Modules:
  0.0 20.9 jit_solution(4628001672615528924)
XLA Ops:
  0.0 19.7 %shard_map.73 = f32[1,2,16]{2,1,0:T(2,128)} custom-call(bf16[1,2,8,1024]{3,2,1,0:T(8,128)(2,1)} %waves_h.1, f32[1,2,16]{2,1,0:T(2,128)} %vector_h.1, f32[1,16]{1,0:T(1,128)} %energies_h.1, bf16[2,1024,1536]{2,1,0:T(8,128)(2,1)} %basis_h.1, f32[32,1536]{1,0:T(8,128)} %screening_h.1, f32[1536]{0:T(1024)} %coulomb_h.1, s32[1,32]{1,0:T(1,128)} %qmap_h.1), custom_call_target="tpu_custom_call" | custom-call | tf_op jit(solution)/shard_map/pallas_call | solution.py:337
  19.7 1.2 %copy.9 = f32[1,2,16]{2,1,0:T(2,128)} copy(f32[1,2,16]{2,1,0:T(2,128)} %shard_map.73) | data formatting | bytes 256

commit v4 on v3

--- a/solution.py
+++ b/solution.py
@@ -51,8 +51,8 @@
     groups, members, n_g,
     waves_h, vector_h, energies_h, basis_h, screening_h, coulomb_h, qmap_h, out,
     vector, energies, coulomb, qmap, basis, screening,
-    stage, team, part, left, weights, weights_in, own_p, pair_p, own_d, s_own, s_in, h_send, h_recv, t_send, t_recv,
-    small_sem, basis_sem, screen_sem, t_ssem, t_rsem, p_ssem, p_rsem, r_ssem, r_rsem,
+    stage, team, part, left, weights, weights_in, own_p, pair_p, own_d, s_own, s_in, h_send, h_recv, t_send, t_recv, d_sum, ex_sum,
+    small_sem, basis_sem, screen_sem, t_ssem, t_rsem, p_ssem, p_rsem, r_ssem,
     w_ssem, w_rsem, s_ssem, s_rsem, h_ssem, h_rsem, d_ssem, d_rsem,
 ):
     offset = groups // 4
@@ -71,12 +71,25 @@
         return who + (s // 2) * (2 - 4 * lax.rem(lax.div(who, 2), 2))
 
     def source(i):
-        if i < half:
-            return lax.rem(kin + members - 2 * i, members)
-        return lax.rem(sib + members - 2 * (i - half), members)
+        relayed = lax.div(i, half)
+        who = kin + relayed * (sib - kin)
+        return lax.rem(who + members - 2 * (i - relayed * half), members)
 
     up = lax.rem(grp + offset, groups)
     down = lax.rem(grp + groups - offset, groups)
+
+    rel_s = [(dg, dt) for dg in range(groups) for dt in range(teams) if (dg, dt) != (0, 0)]
+
+    def s_target(dg, dt):
+        return (lax.rem(grp + dg, groups), lax.rem(kin + dt * TEAM, members))
+
+    barrier = pltpu.get_barrier_semaphore()
+    greet = [s_target(dg, dt) for dg, dt in rel_s] + [(grp, mate(s)) for s in range(1, TEAM)]
+    for dk in range(members):
+        if dk % TEAM:
+            greet += [(up, lax.rem(kin + dk, members)), (down, lax.rem(kin + dk, members))]
+    for target in greet:
+        pl.semaphore_signal(barrier, inc=1, device_id=target, device_id_type=MESH)
 
     my_cols = pl.ds(pl.multiple_of(rank * quarter, 128), quarter)
     pairs = [
@@ -92,19 +105,6 @@
     basis_in = pltpu.make_async_copy(basis_h.at[:, :, my_cols], basis, basis_sem)
     basis_in.start()
 
-    rel_s = [(dg, dt) for dg in range(groups) for dt in range(teams) if (dg, dt) != (0, 0)]
-
-    def s_target(dg, dt):
-        return (lax.rem(grp + dg, groups), lax.rem(kin + dt * TEAM, members))
-
-    barrier = pltpu.get_barrier_semaphore()
-    greet = [s_target(dg, dt) for dg, dt in rel_s] + [(grp, mate(s)) for s in range(1, TEAM)]
-    for dk in range(members):
-        if dk % TEAM:
-            greet += [(up, lax.rem(kin + dk, members)), (down, lax.rem(kin + dk, members))]
-    for target in greet:
-        pl.semaphore_signal(barrier, inc=1, device_id=target, device_id_type=MESH)
-
     for copy in small:
         copy.wait()
     own_vec = vector[0]
@@ -153,18 +153,21 @@
     row8 = iota((8, NT), 0)
     lane8 = iota((8, NT), 1)
 
-    xs = []
     team_in[3] = remote(team.at[2], team.at[3], t_ssem.at[3], t_rsem.at[3], (grp, sib))
-    for s in range(TEAM):
-        if s == 1:
+
+    def team_step(s, carry):
+        @pl.when(s == 1)
+        def _():
             team_in[2].wait_recv()
-            go(team_in[3])
-        if s in (1, 3):
-            team_in[s].wait_recv()
-        src = stage if s == 0 else team.at[s]
-        wre = src[0, :, 0:points].astype(F32)
-        wim = src[1, :, 0:points].astype(F32)
-        xs.append((src[0, :, points:].astype(F32)[0:1, 0:NT], src[1, :, points:].astype(F32)[0:1, 0:NT]))
+            team_in[3].start()
+            team_in[1].wait_recv()
+
+        @pl.when(s == 3)
+        def _():
+            team_in[3].wait_recv()
+
+        wre = team[s, 0, :, 0:points].astype(F32)
+        wim = team[s, 1, :, 0:points].astype(F32)
         cre, cim = twice(wre[NV:]), twice(wim[NV:])
         res, ims = [], []
         for h in range(4):
@@ -178,11 +181,20 @@
                 ims.append(pim)
         pre = jnp.concatenate(res, 0)
         pim = jnp.concatenate(ims, 0)
-        r0 = s * NT
-        own_p[r0:r0 + NT, 0:points] = pre.astype(BF16)
-        own_p[r0:r0 + NT, points:] = (-pim).astype(BF16)
-        own_p[ROWS + r0:ROWS + r0 + NT, 0:points] = pim.astype(BF16)
-        own_p[ROWS + r0:ROWS + r0 + NT, points:] = pre.astype(BF16)
+        re_rows = pl.ds(pl.multiple_of(s * NT, NT), NT)
+        im_rows = pl.ds(pl.multiple_of(ROWS + s * NT, NT), NT)
+        own_p[re_rows, 0:points] = pre.astype(BF16)
+        own_p[re_rows, points:] = (-pim).astype(BF16)
+        own_p[im_rows, 0:points] = pim.astype(BF16)
+        own_p[im_rows, points:] = pre.astype(BF16)
+        return carry
+
+    team[0] = stage[...]
+    lax.fori_loop(0, TEAM, team_step, 0)
+    started.append(team_in[3])
+    xs = []
+    for s in range(TEAM):
+        xs.append((team[s, 0, :, points:].astype(F32)[0:1, 0:NT], team[s, 1, :, points:].astype(F32)[0:1, 0:NT]))
 
     xr = jnp.concatenate([x[0] for x in xs], 1)
     xi = jnp.concatenate([x[1] for x in xs], 1)
@@ -213,17 +225,23 @@
     for s in range(1, TEAM):
         weight_in[s].wait_recv()
 
-    d_re = jnp.zeros((ROWS, side), F32)
-    d_im = jnp.zeros((ROWS, side), F32)
-    exchange = None
-    h_copies = []
-    for i in range(members):
-        if i >= half:
-            part_in[i] = remote(part.at[i - half], part.at[i], r_ssem.at[i - half], r_rsem.at[i - half], (grp, sib))
-        part_in[i].wait_recv()
-        if i < half:
-            go(remote(part.at[i], part.at[half + i], r_ssem.at[i], r_rsem.at[i], (grp, sib)))
-        if i == members - 1:
+    d_sum[...] = jnp.zeros((side, side), F32)
+
+    def relay(i):
+        return remote(part.at[i], part.at[half + i], r_ssem.at[i], p_rsem.at[half + i], (grp, sib))
+
+    def h_copy(i):
+        return remote(h_send.at[i], h_recv.at[i], h_ssem.at[i], h_rsem.at[i], (down, source(i)))
+
+    def partner_step(i, carry):
+        remote(stage, part.at[i], p_ssem.at[0], p_rsem.at[i], (up, kin)).wait_recv()
+
+        @pl.when(i < half)
+        def _():
+            relay(i).start()
+
+        @pl.when(i == members - 1)
+        def _():
             total = s_own[...]
             for j, copy in enumerate(s_copies):
                 copy.wait_recv()
@@ -231,31 +249,34 @@
             pot = coulomb[my_cols].reshape(1, quarter) * total
             ex = mm_nt(jnp.concatenate([hi_lo(pot), jnp.zeros((4, quarter), BF16)], 0), own_d[...])
             ex = ex[0:2] + ex[2:4]
-            exchange = jnp.concatenate(
+            ex_sum[...] = jnp.concatenate(
                 [ex[0:1, 0:ROWS] + ex[1:2, ROWS:], ex[1:2, 0:ROWS] - ex[0:1, ROWS:]], 0)
 
-        slot = i % 2
         wre = part[i, 0, :, 0:points].astype(F32)
         wim = part[i, 1, :, 0:points].astype(F32)
-        for kind in range(2):
-            rows = slice(NV, NV + NC) if kind == 0 else slice(0, NV)
-            rre, rim = twice(wre[rows]), twice(wim[rows])
-            for s in range(TEAM):
+        right = [(twice(wre[NV:]), twice(wim[NV:])), (twice(wre[0:NV]), twice(wim[0:NV]))]
+
+        def product_step(s, carry):
+            for kind in range(2):
                 res, ims = [], []
                 for h in range(2):
                     t = h + 2 - 2 * kind
-                    pre, pim = conj_mul(left[s, t, 0], left[s, t, 1], rre, rim)
+                    pre, pim = conj_mul(left[s, t, 0], left[s, t, 1], *right[kind])
                     res.append(pre)
                     ims.append(pim)
                 pre = jnp.concatenate(res, 0)
                 pim = jnp.concatenate(ims, 0)
-                r0 = kind * side + s * NT
-                pair_p[slot, r0:r0 + NT, 0:points] = pre.astype(BF16)
-                pair_p[slot, r0:r0 + NT, points:] = (-pim).astype(BF16)
-                pair_p[slot, ROWS + r0:ROWS + r0 + NT, 0:points] = pim.astype(BF16)
-                pair_p[slot, ROWS + r0:ROWS + r0 + NT, points:] = pre.astype(BF16)
-
-        dens = mm(pair_p[slot], basis[...].reshape(2 * points, quarter)).astype(BF16)
+                re_rows = pl.ds(pl.multiple_of(kind * side + s * NT, NT), NT)
+                im_rows = pl.ds(pl.multiple_of(kind * side + ROWS + s * NT, NT), NT)
+                pair_p[re_rows, 0:points] = pre.astype(BF16)
+                pair_p[re_rows, points:] = (-pim).astype(BF16)
+                pair_p[im_rows, 0:points] = pim.astype(BF16)
+                pair_p[im_rows, points:] = pre.astype(BF16)
+            return carry
+
+        lax.fori_loop(0, TEAM, product_step, 0)
+
+        dens = mm(pair_p[...], basis[...].reshape(2 * points, quarter)).astype(BF16)
         b = source(i)
         weight = jnp.concatenate(
             [jnp.broadcast_to(weights_in[s, pl.ds(b, 1), :], (NT, quarter)) for s in range(TEAM)] * 2, 0)
@@ -278,7 +299,7 @@
         h_send[i] = jnp.concatenate(
             [jnp.sum(jnp.where(hit, h_sums[0:8], 0.0), 0, keepdims=True),
              jnp.sum(jnp.where(hit, h_sums[8:16], 0.0), 0, keepdims=True)], 0)
-        h_copies.append(go(remote(h_send.at[i], h_recv.at[i], h_ssem.at[i], h_rsem.at[i], (down, b))))
+        h_copy(i).start()
 
         xbr = part[i, 0, :, points:].astype(F32)[:, 0:NT]
         xbi = part[i, 1, :, points:].astype(F32)[:, 0:NT]
@@ -287,11 +308,17 @@
         w2 = jnp.where(first, xx[8:16], xx[0:8])
         w1 = jnp.concatenate([w1] * (ROWS // 8), 0)
         w2 = jnp.concatenate([w2] * (ROWS // 8), 0)
-        d_re = d_re + (k_re * w1 + k_im * w2)
-        d_im = d_im + (k_re * w2 - k_im * w1)
+        d_sum[0:ROWS] += k_re * w1 + k_im * w2
+        d_sum[ROWS:] += k_re * w2 - k_im * w1
+        return carry
+
+    lax.fori_loop(0, members, partner_step, 0)
+    exchange = ex_sum[...]
+    h_copies = [h_copy(i) for i in range(members)]
+    started += [relay(i) for i in range(half)] + h_copies
 
     scale = 1.0 / n_k
-    d_sums = mm_nt(hi_lo(jnp.concatenate([d_re, d_im], 0)), pick_v)
+    d_sums = mm_nt(hi_lo(d_sum[...]), pick_v)
     d_sums = d_sums[0:side] + d_sums[side:]
     d_sums = jnp.where((iota((side, NT), 0) // 4) % 4 == iota((side, NT), 1) % 4, d_sums, 0.0)
     mine = None
@@ -353,7 +380,7 @@
             vmem((members, n_g), F32),
             vmem((TEAM, members, quarter), F32),
             vmem((2 * ROWS, 2 * points), BF16),
-            vmem((2, 4 * ROWS, 2 * points), BF16),
+            vmem((4 * ROWS, 2 * points), BF16),
             vmem((2 * ROWS, quarter), BF16),
             vmem((2, quarter), F32),
             vmem((n_s, 2, quarter), F32),
@@ -361,10 +388,11 @@
             vmem((members, 2, NT), F32),
             vmem((TEAM, 2, NT), F32),
             vmem((TEAM, 2, NT), F32),
+            vmem((2 * ROWS, 2 * ROWS), F32),
+            vmem((2, ROWS), F32),
             dma((5,)), dma, dma,
             dma((TEAM,)), dma((TEAM,)),
-            dma((half,)), dma((half,)),
-            dma((half,)), dma((half,)),
+            dma((half,)), dma((members,)), dma((half,)),
             dma((TEAM,)), dma((TEAM,)),
             dma((n_s,)), dma((n_s,)),
             dma((members,)), dma((members,)),

time: 21.1 us -> 22.1 us (1.047)
  Pallas kernels: 19.7 us -> 20.7 us
    pallas_call x1, Pallas kernels: 19.7 us -> 20.7 us  [on_device(): pl.pallas_call(functools.partial(kernel, groups, members, n_g), out_shape...]
where the time goes in v4:
time: 22.1 us; the launch traced here: 21.9 us
  Pallas kernels  20.7 us (94%)
  local copies, waits for them, and re-layouts  1.24 us (6%)
    pallas_call x1, Pallas kernels, on_device(): pl.pallas_call(functools.partial(kernel, groups, members, n_g), out_shape...  20.7 us
    unnamed x1, local copies, waits for them, and re-layouts  1.24 us

profile of v4, /device:TPU:0, one launch (start us, length us, event | category | flops | bytes accessed | tf_op | source)
XLA Modules:
  0.0 21.9 jit_solution(3078737600537664667)
XLA Ops:
  0.0 20.7 %shard_map.73 = f32[1,2,16]{2,1,0:T(2,128)} custom-call(bf16[1,2,8,1024]{3,2,1,0:T(8,128)(2,1)} %waves_h.1, f32[1,2,16]{2,1,0:T(2,128)} %vector_h.1, f32[1,16]{1,0:T(1,128)} %energies_h.1, bf16[2,1024,1536]{2,1,0:T(8,128)(2,1)} %basis_h.1, f32[32,1536]{1,0:T(8,128)} %screening_h.1, f32[1536]{0:T(1024)} %coulomb_h.1, s32[1,32]{1,0:T(1,128)} %qmap_h.1), custom_call_target="tpu_custom_call" | custom-call | tf_op jit(solution)/shard_map/pallas_call | solution.py:364
  20.7 1.2 %copy.9 = f32[1,2,16]{2,1,0:T(2,128)} copy(f32[1,2,16]{2,1,0:T(2,128)} %shard_map.73) | data formatting | bytes 256

commit v5 on v3

v5 whole, which is shorter than its diff:
```python
import functools

import jax
import jax.numpy as jnp
from jax import lax
from jax.experimental import pallas as pl
from jax.experimental.pallas import tpu as pltpu
from jax.sharding import PartitionSpec as P

NV = 4
NC = 4
NT = 16
TEAM = 2
ROWS = 2 * TEAM * NT
CHUNK = 256
MESH = pl.DeviceIdType.MESH
F32 = jnp.float32
BF16 = jnp.bfloat16


def iota(shape, dim):
    return lax.broadcasted_iota(jnp.int32, shape, dim)


def mm(left, right):
    return jnp.dot(left, right, preferred_element_type=F32)


def mm_nt(left, right):
    return lax.dot_general(left, right, (((1,), (1,)), ((), ())), preferred_element_type=F32)


def hi_lo(value):
    high = value.astype(BF16)
    low = (value - high.astype(F32)).astype(BF16)
    return jnp.concatenate([high, low], 0)


def one_hot(cond):
    return jnp.where(cond, 1.0, 0.0).astype(BF16)


def conj_mul(lre, lim, rre, rim):
    return lre * rre + lim * rim, lre * rim - lim * rre


def twice(rows):
    return jnp.concatenate([rows, rows], 0)


def kernel(
    groups, members, n_g,
    waves_h, vector_h, energies_h, basis_h, screening_h, coulomb_h, qmap_h, out,
    energies, coulomb, qmap, basis, screening, team, team_vec, part, part_vec,
    left, weights, weights_in, own_p, pair_p, own_d, s_own, s_in, s_pair, s_all, h_send, h_recv, t_send, t_recv,
    small_sem, basis_sem, screen_sem, t_ssem, t_rsem, tv_ssem, tv_rsem, p_ssem, p_rsem, pv_ssem, pv_rsem, r_ssem,
    w_ssem, w_rsem, s_ssem, s_rsem, g_ssem, g_rsem, h_ssem, h_rsem, d_ssem, d_rsem,
):
    offset = groups // 4
    half = members // 2
    teams = members // TEAM
    n_k = groups * members
    points = waves_h.shape[3]
    share = n_g // TEAM
    n_chunk = share // CHUNK
    grp = lax.axis_index("grp")
    kin = lax.axis_index("kin")
    rank = lax.rem(kin, TEAM)
    sib = kin + 1 - 2 * rank
    up = lax.rem(grp + offset, groups)
    down = lax.rem(grp + groups - offset, groups)

    def source(i):
        if i < half:
            return lax.rem(kin + members - 2 * i, members)
        return lax.rem(sib + members - 2 * (i - half), members)

    def group_at(dg):
        return (lax.rem(grp + dg, groups), kin)

    def kin_at(g, dk):
        return (g, lax.rem(kin + dk, members))

    greet = [kin_at(g, dk) for g in (up, down) for dk in range(1, members)]
    greet += [group_at(dg) for dg in range(1, groups)] + [kin_at(grp, dk) for dk in range(1, members)]
    barrier = pltpu.get_barrier_semaphore()
    for target in greet:
        pl.semaphore_signal(barrier, inc=1, device_id=target, device_id_type=MESH)

    my_cols = pl.ds(pl.multiple_of(rank * share, 128), share)
    pairs = [
        (waves_h, team.at[pl.ds(0, 1)]), (vector_h, team_vec.at[pl.ds(0, 1)]), (qmap_h, qmap),
        (energies_h, energies), (coulomb_h, coulomb),
    ]
    small = []
    for i, (src, dst) in enumerate(pairs):
        small.append(pltpu.make_async_copy(src, dst, small_sem.at[i]))
        small[-1].start()
    basis_in = []
    for n in range(n_chunk):
        src = pl.ds(pl.multiple_of(rank * share + n * CHUNK, 128), CHUNK)
        basis_in.append(pltpu.make_async_copy(
            basis_h.at[:, :, src], basis.at[:, :, pl.ds(n * CHUNK, CHUNK)], basis_sem.at[n]))
        basis_in[-1].start()
        if n == 0:
            screen_in = pltpu.make_async_copy(screening_h, screening, screen_sem)
            screen_in.start()
    pl.semaphore_wait(barrier, len(greet))

    started = []

    def send(src, dst, ssem, rsem, target):
        copy = pltpu.make_async_remote_copy(
            src_ref=src, dst_ref=dst, send_sem=ssem, recv_sem=rsem, device_id=target, device_id_type=MESH
        )
        copy.start()
        started.append(copy)
        return copy

    one = pl.ds(1, 1)
    part_in = [None] * members
    for i in range(half):
        part_in[i] = send(waves_h, part.at[pl.ds(i, 1)], p_ssem.at[i], p_rsem.at[i], kin_at(up, 2 * i))
    team_in = send(waves_h, team.at[one], t_ssem, t_rsem, (grp, sib))
    team_vec_in = send(vector_h, team_vec.at[one], tv_ssem, tv_rsem, (grp, sib))
    vec_in = []
    for i in range(members):
        if i < half:
            target = kin_at(up, 2 * i)
        else:
            target = (up, lax.rem(sib + 2 * (i - half), members))
        vec_in.append(send(vector_h, part_vec.at[pl.ds(i, 1)], pv_ssem.at[i], pv_rsem.at[i], target))

    for copy in small:
        copy.wait()
    low_half = iota((8, points), 0) < 4
    re_rows, im_rows = slice(0, ROWS), slice(ROWS, 2 * ROWS)

    def team_part(s):
        wre = team[s, 0].astype(F32)
        wim = team[s, 1].astype(F32)
        cre, cim = twice(wre[NV:]), twice(wim[NV:])
        res, ims = [], []
        for h in range(4):
            lre = jnp.where(low_half, wre[2 * h:2 * h + 1], wre[2 * h + 1:2 * h + 2])
            lim = jnp.where(low_half, wim[2 * h:2 * h + 1], wim[2 * h + 1:2 * h + 2])
            left[s, h, 0] = lre
            left[s, h, 1] = lim
            if h < 2:
                pre, pim = conj_mul(lre, lim, cre, cim)
                res.append(pre)
                ims.append(pim)
        pre = jnp.concatenate(res, 0)
        pim = jnp.concatenate(ims, 0)
        r0 = s * NT
        r1 = TEAM * NT + s * NT
        own_p[r0:r0 + NT, 0:points] = pre.astype(BF16)
        own_p[r0:r0 + NT, points:] = (-pim).astype(BF16)
        own_p[r1:r1 + NT, 0:points] = pim.astype(BF16)
        own_p[r1:r1 + NT, points:] = pre.astype(BF16)

    team_part(0)

    side = 2 * ROWS
    col = iota((NT, side), 1)
    tr = iota((NT, side), 0)
    pick_v = one_hot((col // 4) % 4 == tr // 4)
    pick_w = one_hot(col % 4 == tr // 4)
    same = (iota((side, side), 0) // NT) % 4 == (iota((side, side), 1) // NT) % 4
    first = iota((8, side), 1) < ROWS
    row8 = iota((8, NT), 0)
    lane8 = iota((8, NT), 1)
    hit_d = row8 % 4 == lane8 % 4

    screen_in.wait()
    base = down * members
    for b in range(members):
        weights[b:b + 1, :] = screening[pl.ds(qmap[0, base + b], 1), :]
    sib_cols = pl.ds(pl.multiple_of((1 - rank) * share, 128), share)
    weight_in = send(weights.at[:, sib_cols], weights_in.at[1], w_ssem, w_rsem, (grp, sib))
    weights_in[0] = weights[:, my_cols]

    team_in.wait_recv()
    team_vec_in.wait_recv()
    team_part(1)
    xs = []
    for s in range(TEAM):
        x = team_vec[s].astype(BF16).astype(F32)
        xs.append((x[0:1], x[1:2]))
    xr = jnp.concatenate([x[0] for x in xs], 1)
    xi = jnp.concatenate([x[1] for x in xs], 1)
    x_rows = jnp.concatenate(
        [jnp.concatenate([xr, -xi], 1), jnp.concatenate([xi, xr], 1), jnp.zeros((6, 2 * TEAM * NT), F32)], 0
    ).astype(BF16)

    def basis_cols(n):
        return basis[:, :, n * CHUNK:(n + 1) * CHUNK].reshape(2 * points, CHUNK)

    for n in range(n_chunk):
        basis_in[n].wait()
        cols = slice(n * CHUNK, (n + 1) * CHUNK)
        dens = mm(own_p[...], basis_cols(n)).astype(BF16)
        own_d[:, cols] = dens
        s_own[:, cols] = mm(x_rows, dens)[0:2]
    s_copies = []
    for i in range(teams - 1):
        s_copies.append(send(s_own, s_in.at[i], s_ssem.at[i], s_rsem.at[i], kin_at(grp, TEAM * (i + 1))))

    a_re, a_im = [], []
    for s in range(TEAM):
        for c in range(0, NC, 2):
            hit = lane8 % 4 == c + row8 // 4
            a_re.append(jnp.where(hit, xs[s][0], 0.0))
            a_im.append(jnp.where(hit, xs[s][1], 0.0))
    spread = mm(jnp.concatenate(a_re + a_im, 0).astype(BF16), pick_v)
    first_32 = iota((TEAM * NT, side), 1) < ROWS
    a_re, a_im = spread[0:TEAM * NT], spread[TEAM * NT:]
    u1 = twice(jnp.where(first_32, a_re, a_im))
    u2 = twice(jnp.where(first_32, -a_im, a_re))

    def products(i, batch, j):
        wre = part[i, 0].astype(F32)
        wim = part[i, 1].astype(F32)
        for kind in range(2):
            bands = slice(NV, NV + NC) if kind == 0 else slice(0, NV)
            rre, rim = twice(wre[bands]), twice(wim[bands])
            for s in range(TEAM):
                res, ims = [], []
                for h in range(2):
                    t = h + 2 - 2 * kind
                    pre, pim = conj_mul(left[s, t, 0], left[s, t, 1], rre, rim)
                    res.append(pre)
                    ims.append(pim)
                pre = jnp.concatenate(res, 0)
                pim = jnp.concatenate(ims, 0)
                r0 = kind * side + j * TEAM * NT + s * NT
                r1 = r0 + ROWS
                pair_p[batch, r0:r0 + NT, 0:points] = pre.astype(BF16)
                pair_p[batch, r0:r0 + NT, points:] = (-pim).astype(BF16)
                pair_p[batch, r1:r1 + NT, 0:points] = pim.astype(BF16)
                pair_p[batch, r1:r1 + NT, points:] = pre.astype(BF16)

    def kernel_of(batch):
        total = None
        for n in range(n_chunk):
            cols = slice(n * CHUNK, (n + 1) * CHUNK)
            dens = mm(pair_p[batch % 2], basis_cols(n)).astype(BF16)
            rows = []
            for j in range(2):
                b = source(2 * batch + j)
                rows += [jnp.broadcast_to(weights_in[s, pl.ds(b, 1), cols], (NT, CHUNK)) for s in range(TEAM)]
            weight = jnp.concatenate(rows * 2, 0)
            cond = (dens[0:side].astype(F32) * weight).astype(BF16)
            term = mm_nt(cond, dens[side:])
            total = term if total is None else total + term
        return jnp.where(same, total, 0.0)

    kerns = []
    for batch in range(members // 2):
        for i in (2 * batch, 2 * batch + 1):
            if i >= half:
                k = pl.ds(i, 1)
                part_in[i] = pltpu.make_async_remote_copy(
                    src_ref=part.at[k], dst_ref=part.at[k], send_sem=r_ssem.at[i - half], recv_sem=p_rsem.at[i],
                    device_id=(grp, sib), device_id_type=MESH)
            part_in[i].wait_recv()
            if i < half:
                send(part.at[i], part.at[half + i], r_ssem.at[i], p_rsem.at[half + i], (grp, sib))
        if batch == 0:
            weight_in.wait_recv()
        for j in range(2):
            products(2 * batch + j, batch % 2, j)
        kerns.append(kernel_of(batch))
        if batch == 0:
            total = s_own[...]
            for i, copy in enumerate(s_copies):
                copy.wait_recv()
                total = total + s_in[i]
            s_pair[...] = total
            g_copies = []
            for i in range(groups - 1):
                g_copies.append(send(s_pair, s_all.at[i], g_ssem.at[i], g_rsem.at[i], group_at(i + 1)))

    h_rows = []
    for kern in kerns:
        k_re, k_im = kern[re_rows], kern[im_rows]
        for value in (k_re * u1 + k_im * u2, k_im * u1 - k_re * u2):
            for j in range(2):
                r0 = j * TEAM * NT
                h_rows.append(value[r0:r0 + 8] + value[r0 + 8:r0 + 16] + value[r0 + 16:r0 + 24] + value[r0 + 24:r0 + 32])
    n_h = 8 * len(h_rows)
    h_sums = mm_nt(hi_lo(jnp.concatenate(h_rows, 0)), pick_w)
    h_sums = h_sums[0:n_h] + h_sums[n_h:]

    def h_row(batch, comp, j):
        r0 = 8 * (4 * batch + 2 * comp + j)
        return jnp.sum(jnp.where(hit_d, h_sums[r0:r0 + 8], 0.0), 0, keepdims=True)

    h_copies = []
    for i in range(members):
        h_send[i] = jnp.concatenate([h_row(i // 2, 0, i % 2), h_row(i // 2, 1, i % 2)], 0)
    for i in range(members):
        h_copies.append(send(h_send.at[i], h_recv.at[i], h_ssem.at[i], h_rsem.at[i], (down, source(i))))

    for copy in vec_in:
        copy.wait_recv()
    d_re = jnp.zeros((ROWS, side), F32)
    d_im = jnp.zeros((ROWS, side), F32)
    for batch, kern in enumerate(kerns):
        k_re, k_im = kern[re_rows], kern[im_rows]
        x_parts = []
        for j in range(2):
            xb = part_vec[2 * batch + j].astype(BF16).astype(F32)
            x_parts += [jnp.where(hit_d, xb[0:1], 0.0), jnp.where(hit_d, xb[1:2], 0.0)]
        xx = mm(jnp.concatenate(x_parts, 0).astype(BF16), pick_w)
        w1, w2 = [], []
        for j in range(2):
            x_re, x_im = xx[16 * j:16 * j + 8], xx[16 * j + 8:16 * j + 16]
            w1 += [jnp.where(first, x_re, -x_im)] * (2 * TEAM)
            w2 += [jnp.where(first, x_im, x_re)] * (2 * TEAM)
        w1 = jnp.concatenate(w1, 0)
        w2 = jnp.concatenate(w2, 0)
        d_re = d_re + (k_re * w1 + k_im * w2)
        d_im = d_im + (k_re * w2 - k_im * w1)
    n_d = TEAM * NT
    d_rows = jnp.concatenate([d_re[0:n_d] + d_re[n_d:], d_im[0:n_d] + d_im[n_d:]], 0)
    d_sums = mm_nt(hi_lo(d_rows), pick_v)
    d_sums = d_sums[0:2 * n_d] + d_sums[2 * n_d:]
    d_sums = jnp.where((iota((2 * n_d, NT), 0) // 4) % 4 == iota((2 * n_d, NT), 1) % 4, d_sums, 0.0)

    total = s_pair[...]
    for i, copy in enumerate(g_copies):
        copy.wait_recv()
        total = total + s_all[i]
    pot = coulomb[my_cols].reshape(1, share) * total
    ex = mm_nt(jnp.concatenate([hi_lo(pot), jnp.zeros((4, share), BF16)], 0), own_d[...])
    ex = ex[0:2] + ex[2:4]
    exchange = jnp.concatenate([ex[0:1, 0:n_d] + ex[1:2, n_d:], ex[1:2, 0:n_d] - ex[0:1, n_d:]], 0)

    scale = 1.0 / n_k
    sums = []
    for s in range(TEAM):
        direct = jnp.concatenate(
            [jnp.sum(d_sums[r:r + NT], 0, keepdims=True) for r in (s * NT, n_d + s * NT)], 0)
        sums.append((2.0 * scale) * exchange[:, s * NT:(s + 1) * NT] - scale * direct)
    t_send[...] = sums[1]
    d_copy = send(t_send, t_recv, d_ssem, d_rsem, (grp, sib))
    result = energies[...] * team_vec[0] + sums[0]
    for copy in h_copies:
        copy.wait_recv()
    back = h_recv[0]
    for i in range(1, members):
        back = back + h_recv[i]
    d_copy.wait_recv()
    out[0] = result + t_recv[...] - scale * back

    for copy in started:
        copy.wait_send()


def on_device(waves, vector, energies, basis, screening, coulomb, qmap):
    groups = lax.axis_size("grp")
    members = lax.axis_size("kin")
    half = members // 2
    points = waves.shape[3]
    n_g = basis.shape[2]
    share = n_g // TEAM
    n_s = max(members // TEAM - 1, 1)
    any_space = pl.BlockSpec(memory_space=pl.ANY)
    dma = pltpu.SemaphoreType.DMA
    vmem = pltpu.VMEM
    n_own = 2 * TEAM * NT
    return pl.pallas_call(
        functools.partial(kernel, groups, members, n_g),
        out_shape=jax.ShapeDtypeStruct(vector.shape, F32),
        in_specs=[any_space] * 7,
        out_specs=pl.BlockSpec(memory_space=vmem),
        scratch_shapes=[
            vmem(energies.shape, F32),
            vmem(coulomb.shape, F32),
            pltpu.SMEM(qmap.shape, jnp.int32),
            vmem((2, points, share), BF16),
            vmem(screening.shape, F32),
            vmem((TEAM,) + waves.shape[1:], BF16),
            vmem((TEAM, 2, NT), F32),
            vmem((members,) + waves.shape[1:], BF16),
            vmem((members, 2, NT), F32),
            vmem((TEAM, 4, 2, 8, points), F32),
            vmem((members, n_g), F32),
            vmem((TEAM, members, share), F32),
            vmem((n_own, 2 * points), BF16),
            vmem((2, 4 * ROWS, 2 * points), BF16),
            vmem((n_own, share), BF16),
            vmem((2, share), F32),
            vmem((n_s, 2, share), F32),
            vmem((2, share), F32),
            vmem((groups - 1, 2, share), F32),
            vmem((members, 2, NT), F32),
            vmem((members, 2, NT), F32),
            vmem((2, NT), F32),
            vmem((2, NT), F32),
            dma((5,)), dma((share // CHUNK,)), dma,
            dma, dma, dma, dma,
            dma((half,)), dma((members,)),
            dma((members,)), dma((members,)),
            dma((half,)),
            dma, dma,
            dma((n_s,)), dma((n_s,)),
            dma((groups - 1,)), dma((groups - 1,)),
            dma((members,)), dma((members,)),
            dma, dma,
        ],
        compiler_params=pltpu.CompilerParams(
            collective_id=0, has_side_effects=True, vmem_limit_bytes=60 * 1024 * 1024
        ),
    )(waves, vector, energies, basis, screening, coulomb, qmap)


def solution(mesh):
    return jax.shard_map(
        on_device,
        mesh=mesh,
        in_specs=(
            P(("grp", "kin"), None, None, None),
            P(("grp", "kin"), None, None),
            P(("grp", "kin"), None),
            P(),
            P(),
            P(),
            P(("grp", "kin"), None),
        ),
        out_specs=P(("grp", "kin"), None, None),
        check_vma=False,
    )
```

time: 21.1 us -> 19.1 us (0.905)
  Pallas kernels: 19.7 us -> 17.7 us
    pallas_call x1, Pallas kernels: 19.7 us -> 17.7 us  [on_device(): pl.pallas_call(functools.partial(kernel, groups, members, n_g), out_shape...]
where the time goes in v5:
time: 19.1 us; the launch traced here: 19 us
  Pallas kernels  17.7 us (93%)
  local copies, waits for them, and re-layouts  1.24 us (6%)
    pallas_call x1, Pallas kernels, on_device(): pl.pallas_call(functools.partial(kernel, groups, members, n_g), out_shape...  17.7 us
    unnamed x1, local copies, waits for them, and re-layouts  1.24 us

profile of v5, /device:TPU:0, one launch (start us, length us, event | category | flops | bytes accessed | tf_op | source)
XLA Modules:
  0.0 19.0 jit_solution(14433181361132855032)
XLA Ops:
  0.0 17.7 %shard_map.73 = f32[1,2,16]{2,1,0:T(2,128)} custom-call(bf16[1,2,8,1024]{3,2,1,0:T(8,128)(2,1)} %waves_h.1, f32[1,2,16]{2,1,0:T(2,128)} %vector_h.1, f32[1,16]{1,0:T(1,128)} %energies_h.1, bf16[2,1024,1536]{2,1,0:T(8,128)(2,1)} %basis_h.1, f32[32,1536]{1,0:T(8,128)} %screening_h.1, f32[1536]{0:T(1024)} %coulomb_h.1, s32[1,32]{1,0:T(1,128)} %qmap_h.1), custom_call_target="tpu_custom_call" | custom-call | tf_op jit(solution)/shard_map/pallas_call | solution.py:373
  17.7 1.2 %copy.9 = f32[1,2,16]{2,1,0:T(2,128)} copy(f32[1,2,16]{2,1,0:T(2,128)} %shard_map.73) | data formatting | bytes 256

commit v6 on v5

--- a/solution.py
+++ b/solution.py
@@ -52,8 +52,8 @@
     groups, members, n_g,
     waves_h, vector_h, energies_h, basis_h, screening_h, coulomb_h, qmap_h, out,
     energies, coulomb, qmap, basis, screening, team, team_vec, part, part_vec,
-    left, weights, weights_in, own_p, pair_p, own_d, s_own, s_in, s_pair, s_all, h_send, h_recv, t_send, t_recv,
-    small_sem, basis_sem, screen_sem, t_ssem, t_rsem, tv_ssem, tv_rsem, p_ssem, p_rsem, pv_ssem, pv_rsem, r_ssem,
+    left, weights, weights_in, own_p, pair_a, pair_b, own_d, s_own, s_in, s_pair, s_all, h_send, h_recv, t_send, t_recv,
+    small_sem, basis_sem, screen_sem, t_ssem, t_rsem, tv_ssem, tv_rsem, p_ssem, p_rsem, pv_ssem, pv_rsem,
     w_ssem, w_rsem, s_ssem, s_rsem, g_ssem, g_rsem, h_ssem, h_rsem, d_ssem, d_rsem,
 ):
     offset = groups // 4
@@ -118,17 +118,15 @@
         return copy
 
     one = pl.ds(1, 1)
-    part_in = [None] * members
-    for i in range(half):
-        part_in[i] = send(waves_h, part.at[pl.ds(i, 1)], p_ssem.at[i], p_rsem.at[i], kin_at(up, 2 * i))
+    targets = [kin_at(up, 2 * i) for i in range(half)]
+    targets += [(up, lax.rem(sib + 2 * i, members)) for i in range(half)]
+    part_in = []
     team_in = send(waves_h, team.at[one], t_ssem, t_rsem, (grp, sib))
     team_vec_in = send(vector_h, team_vec.at[one], tv_ssem, tv_rsem, (grp, sib))
+    for i, target in enumerate(targets):
+        part_in.append(send(waves_h, part.at[pl.ds(i, 1)], p_ssem.at[i], p_rsem.at[i], target))
     vec_in = []
-    for i in range(members):
-        if i < half:
-            target = kin_at(up, 2 * i)
-        else:
-            target = (up, lax.rem(sib + 2 * (i - half), members))
+    for i, target in enumerate(targets):
         vec_in.append(send(vector_h, part_vec.at[pl.ds(i, 1)], pv_ssem.at[i], pv_rsem.at[i], target))
 
     for copy in small:
@@ -218,7 +216,7 @@
     u1 = twice(jnp.where(first_32, a_re, a_im))
     u2 = twice(jnp.where(first_32, -a_im, a_re))
 
-    def products(i, batch, j):
+    def products(i, pair_p, j):
         wre = part[i, 0].astype(F32)
         wim = part[i, 1].astype(F32)
         for kind in range(2):
@@ -235,16 +233,16 @@
                 pim = jnp.concatenate(ims, 0)
                 r0 = kind * side + j * TEAM * NT + s * NT
                 r1 = r0 + ROWS
-                pair_p[batch, r0:r0 + NT, 0:points] = pre.astype(BF16)
-                pair_p[batch, r0:r0 + NT, points:] = (-pim).astype(BF16)
-                pair_p[batch, r1:r1 + NT, 0:points] = pim.astype(BF16)
-                pair_p[batch, r1:r1 + NT, points:] = pre.astype(BF16)
-
-    def kernel_of(batch):
+                pair_p[r0:r0 + NT, 0:points] = pre.astype(BF16)
+                pair_p[r0:r0 + NT, points:] = (-pim).astype(BF16)
+                pair_p[r1:r1 + NT, 0:points] = pim.astype(BF16)
+                pair_p[r1:r1 + NT, points:] = pre.astype(BF16)
+
+    def kernel_of(batch, pair_p):
         total = None
         for n in range(n_chunk):
             cols = slice(n * CHUNK, (n + 1) * CHUNK)
-            dens = mm(pair_p[batch % 2], basis_cols(n)).astype(BF16)
+            dens = mm(pair_p[...], basis_cols(n)).astype(BF16)
             rows = []
             for j in range(2):
                 b = source(2 * batch + j)
@@ -255,31 +253,30 @@
             total = term if total is None else total + term
         return jnp.where(same, total, 0.0)
 
+    weight_in.wait_recv()
+    for copy in part_in + vec_in:
+        copy.wait_recv()
+    pairs_of = (pair_a, pair_b)
+
+    def both_products(batch):
+        for j in range(2):
+            products(2 * batch + j, pairs_of[batch % 2], j)
+
+    both_products(0)
+    total = s_own[...]
+    for i, copy in enumerate(s_copies):
+        copy.wait_recv()
+        total = total + s_in[i]
+    s_pair[...] = total
+    g_copies = []
+    for i in range(groups - 1):
+        g_copies.append(send(s_pair, s_all.at[i], g_ssem.at[i], g_rsem.at[i], group_at(i + 1)))
+
     kerns = []
-    for batch in range(members // 2):
-        for i in (2 * batch, 2 * batch + 1):
-            if i >= half:
-                k = pl.ds(i, 1)
-                part_in[i] = pltpu.make_async_remote_copy(
-                    src_ref=part.at[k], dst_ref=part.at[k], send_sem=r_ssem.at[i - half], recv_sem=p_rsem.at[i],
-                    device_id=(grp, sib), device_id_type=MESH)
-            part_in[i].wait_recv()
-            if i < half:
-                send(part.at[i], part.at[half + i], r_ssem.at[i], p_rsem.at[half + i], (grp, sib))
-        if batch == 0:
-            weight_in.wait_recv()
-        for j in range(2):
-            products(2 * batch + j, batch % 2, j)
-        kerns.append(kernel_of(batch))
-        if batch == 0:
-            total = s_own[...]
-            for i, copy in enumerate(s_copies):
-                copy.wait_recv()
-                total = total + s_in[i]
-            s_pair[...] = total
-            g_copies = []
-            for i in range(groups - 1):
-                g_copies.append(send(s_pair, s_all.at[i], g_ssem.at[i], g_rsem.at[i], group_at(i + 1)))
+    for batch in range(half):
+        if batch + 1 < half:
+            both_products(batch + 1)
+        kerns.append(kernel_of(batch, pairs_of[batch % 2]))
 
     h_rows = []
     for kern in kerns:
@@ -299,11 +296,6 @@
     h_copies = []
     for i in range(members):
         h_send[i] = jnp.concatenate([h_row(i // 2, 0, i % 2), h_row(i // 2, 1, i % 2)], 0)
-    for i in range(members):
-        h_copies.append(send(h_send.at[i], h_recv.at[i], h_ssem.at[i], h_rsem.at[i], (down, source(i))))
-
-    for copy in vec_in:
-        copy.wait_recv()
     d_re = jnp.zeros((ROWS, side), F32)
     d_im = jnp.zeros((ROWS, side), F32)
     for batch, kern in enumerate(kerns):
@@ -328,6 +320,9 @@
     d_sums = d_sums[0:2 * n_d] + d_sums[2 * n_d:]
     d_sums = jnp.where((iota((2 * n_d, NT), 0) // 4) % 4 == iota((2 * n_d, NT), 1) % 4, d_sums, 0.0)
 
+    for i in range(members):
+        h_copies.append(send(h_send.at[i], h_recv.at[i], h_ssem.at[i], h_rsem.at[i], (down, source(i))))
+
     total = s_pair[...]
     for i, copy in enumerate(g_copies):
         copy.wait_recv()
@@ -346,6 +341,8 @@
     t_send[...] = sums[1]
     d_copy = send(t_send, t_recv, d_ssem, d_rsem, (grp, sib))
     result = energies[...] * team_vec[0] + sums[0]
+    for copy in started:
+        copy.wait_send()
     for copy in h_copies:
         copy.wait_recv()
     back = h_recv[0]
@@ -353,9 +350,6 @@
         back = back + h_recv[i]
     d_copy.wait_recv()
     out[0] = result + t_recv[...] - scale * back
-
-    for copy in started:
-        copy.wait_send()
 
 
 def on_device(waves, vector, energies, basis, screening, coulomb, qmap):
@@ -389,7 +383,8 @@
             vmem((members, n_g), F32),
             vmem((TEAM, members, share), F32),
             vmem((n_own, 2 * points), BF16),
-            vmem((2, 4 * ROWS, 2 * points), BF16),
+            vmem((4 * ROWS, 2 * points), BF16),
+            vmem((4 * ROWS, 2 * points), BF16),
             vmem((n_own, share), BF16),
             vmem((2, share), F32),
             vmem((n_s, 2, share), F32),
@@ -401,9 +396,8 @@
             vmem((2, NT), F32),
             dma((5,)), dma((share // CHUNK,)), dma,
             dma, dma, dma, dma,
-            dma((half,)), dma((members,)),
             dma((members,)), dma((members,)),
-            dma((half,)),
+            dma((members,)), dma((members,)),
             dma, dma,
             dma((n_s,)), dma((n_s,)),
             dma((groups - 1,)), dma((groups - 1,)),

time: 19.1 us -> 20.5 us (1.073)
  Pallas kernels: 17.7 us -> 19.1 us
    pallas_call x1, Pallas kernels: 17.7 us -> 19.1 us  [on_device(): pl.pallas_call(functools.partial(kernel, groups, members, n_g), out_shape...]
where the time goes in v6:
time: 20.5 us; the launch traced here: 20.3 us
  Pallas kernels  19.1 us (93%)
  local copies, waits for them, and re-layouts  1.24 us (6%)
    pallas_call x1, Pallas kernels, on_device(): pl.pallas_call(functools.partial(kernel, groups, members, n_g), out_shape...  19.1 us
    unnamed x1, local copies, waits for them, and re-layouts  1.24 us

profile of v6, /device:TPU:0, one launch (start us, length us, event | category | flops | bytes accessed | tf_op | source)
XLA Modules:
  0.0 20.3 jit_solution(16294283492543713975)
XLA Ops:
  0.0 19.1 %shard_map.73 = f32[1,2,16]{2,1,0:T(2,128)} custom-call(bf16[1,2,8,1024]{3,2,1,0:T(8,128)(2,1)} %waves_h.1, f32[1,2,16]{2,1,0:T(2,128)} %vector_h.1, f32[1,16]{1,0:T(1,128)} %energies_h.1, bf16[2,1024,1536]{2,1,0:T(8,128)(2,1)} %basis_h.1, f32[32,1536]{1,0:T(8,128)} %screening_h.1, f32[1536]{0:T(1024)} %coulomb_h.1, s32[1,32]{1,0:T(1,128)} %qmap_h.1), custom_call_target="tpu_custom_call" | custom-call | tf_op jit(solution)/shard_map/pallas_call | solution.py:367
  19.1 1.2 %copy.9 = f32[1,2,16]{2,1,0:T(2,128)} copy(f32[1,2,16]{2,1,0:T(2,128)} %shard_map.73) | data formatting | bytes 256

commit v7 on v6

--- a/solution.py
+++ b/solution.py
@@ -52,7 +52,7 @@
     groups, members, n_g,
     waves_h, vector_h, energies_h, basis_h, screening_h, coulomb_h, qmap_h, out,
     energies, coulomb, qmap, basis, screening, team, team_vec, part, part_vec,
-    left, weights, weights_in, own_p, pair_a, pair_b, own_d, s_own, s_in, s_pair, s_all, h_send, h_recv, t_send, t_recv,
+    left, weights, weights_in, own_p, pair_a, pair_b, own_d, s_own, s_in, s_plane, s_all, h_send, h_recv, t_send, t_recv,
     small_sem, basis_sem, screen_sem, t_ssem, t_rsem, tv_ssem, tv_rsem, p_ssem, p_rsem, pv_ssem, pv_rsem,
     w_ssem, w_rsem, s_ssem, s_rsem, g_ssem, g_rsem, h_ssem, h_rsem, d_ssem, d_rsem,
 ):
@@ -78,11 +78,16 @@
     def group_at(dg):
         return (lax.rem(grp + dg, groups), kin)
 
+    def spot_at(ds, dk):
+        level = lax.div(grp, offset)
+        return kin_at(level * offset + lax.rem(grp - level * offset + ds, offset), dk)
+
     def kin_at(g, dk):
         return (g, lax.rem(kin + dk, members))
 
-    greet = [kin_at(g, dk) for g in (up, down) for dk in range(1, members)]
-    greet += [group_at(dg) for dg in range(1, groups)] + [kin_at(grp, dk) for dk in range(1, members)]
+    plane = [(ds, dt) for ds in range(offset) for dt in range(teams) if (ds, dt) != (0, 0)]
+    plane_at = [spot_at(ds, TEAM * dt) for ds, dt in plane]
+    greet = [kin_at(g, dk) for g in (up, down) for dk in range(members)] + [group_at(2 * offset), (grp, sib)] + plane_at
     barrier = pltpu.get_barrier_semaphore()
     for target in greet:
         pl.semaphore_signal(barrier, inc=1, device_id=target, device_id_type=MESH)
@@ -120,11 +125,9 @@
     one = pl.ds(1, 1)
     targets = [kin_at(up, 2 * i) for i in range(half)]
     targets += [(up, lax.rem(sib + 2 * i, members)) for i in range(half)]
-    part_in = []
+    part_in = [send(waves_h, part.at[pl.ds(0, 1)], p_ssem.at[0], p_rsem.at[0], kin_at(up, 0))]
     team_in = send(waves_h, team.at[one], t_ssem, t_rsem, (grp, sib))
     team_vec_in = send(vector_h, team_vec.at[one], tv_ssem, tv_rsem, (grp, sib))
-    for i, target in enumerate(targets):
-        part_in.append(send(waves_h, part.at[pl.ds(i, 1)], p_ssem.at[i], p_rsem.at[i], target))
     vec_in = []
     for i, target in enumerate(targets):
         vec_in.append(send(vector_h, part_vec.at[pl.ds(i, 1)], pv_ssem.at[i], pv_rsem.at[i], target))
@@ -181,6 +184,17 @@
     team_in.wait_recv()
     team_vec_in.wait_recv()
     team_part(1)
+
+    part_in[0].wait_recv()
+    sib_in = [send(part.at[0], part.at[half], p_ssem.at[half], p_rsem.at[half], (grp, sib))]
+    for i in range(1, half):
+        part_in.append(send(part.at[0], part.at[i], p_ssem.at[i], p_rsem.at[i], kin_at(grp, 2 * i)))
+
+    def pass_on():
+        for i in range(1, half):
+            part_in[i].wait_recv()
+            sib_in.append(send(part.at[i], part.at[half + i], p_ssem.at[half + i], p_rsem.at[half + i], (grp, sib)))
+
     xs = []
     for s in range(TEAM):
         x = team_vec[s].astype(BF16).astype(F32)
@@ -195,14 +209,16 @@
         return basis[:, :, n * CHUNK:(n + 1) * CHUNK].reshape(2 * points, CHUNK)
 
     for n in range(n_chunk):
+        if n == n_chunk - 1:
+            pass_on()
         basis_in[n].wait()
         cols = slice(n * CHUNK, (n + 1) * CHUNK)
         dens = mm(own_p[...], basis_cols(n)).astype(BF16)
         own_d[:, cols] = dens
         s_own[:, cols] = mm(x_rows, dens)[0:2]
     s_copies = []
-    for i in range(teams - 1):
-        s_copies.append(send(s_own, s_in.at[i], s_ssem.at[i], s_rsem.at[i], kin_at(grp, TEAM * (i + 1))))
+    for i, target in enumerate(plane_at):
+        s_copies.append(send(s_own, s_in.at[i], s_ssem.at[i], s_rsem.at[i], target))
 
     a_re, a_im = [], []
     for s in range(TEAM):
@@ -245,7 +261,7 @@
             dens = mm(pair_p[...], basis_cols(n)).astype(BF16)
             rows = []
             for j in range(2):
-                b = source(2 * batch + j)
+                b = source(j * half + batch)
                 rows += [jnp.broadcast_to(weights_in[s, pl.ds(b, 1), cols], (NT, CHUNK)) for s in range(TEAM)]
             weight = jnp.concatenate(rows * 2, 0)
             cond = (dens[0:side].astype(F32) * weight).astype(BF16)
@@ -254,29 +270,31 @@
         return jnp.where(same, total, 0.0)
 
     weight_in.wait_recv()
-    for copy in part_in + vec_in:
-        copy.wait_recv()
+    sib_in[0].wait_recv()
     pairs_of = (pair_a, pair_b)
 
     def both_products(batch):
         for j in range(2):
-            products(2 * batch + j, pairs_of[batch % 2], j)
+            products(j * half + batch, pairs_of[batch % 2], j)
 
     both_products(0)
     total = s_own[...]
     for i, copy in enumerate(s_copies):
         copy.wait_recv()
         total = total + s_in[i]
-    s_pair[...] = total
+    s_plane[...] = total
     g_copies = []
-    for i in range(groups - 1):
-        g_copies.append(send(s_pair, s_all.at[i], g_ssem.at[i], g_rsem.at[i], group_at(i + 1)))
+    for i in range(3):
+        g_copies.append(send(s_plane, s_all.at[i], g_ssem.at[i], g_rsem.at[i], group_at(offset * (i + 1))))
 
     kerns = []
     for batch in range(half):
+        kerns.append(kernel_of(batch, pairs_of[batch % 2]))
         if batch + 1 < half:
+            sib_in[batch + 1].wait_recv()
             both_products(batch + 1)
-        kerns.append(kernel_of(batch, pairs_of[batch % 2]))
+    for copy in vec_in:
+        copy.wait_recv()
 
     h_rows = []
     for kern in kerns:
@@ -295,14 +313,14 @@
 
     h_copies = []
     for i in range(members):
-        h_send[i] = jnp.concatenate([h_row(i // 2, 0, i % 2), h_row(i // 2, 1, i % 2)], 0)
+        h_send[i] = jnp.concatenate([h_row(i % half, 0, i // half), h_row(i % half, 1, i // half)], 0)
     d_re = jnp.zeros((ROWS, side), F32)
     d_im = jnp.zeros((ROWS, side), F32)
     for batch, kern in enumerate(kerns):
         k_re, k_im = kern[re_rows], kern[im_rows]
         x_parts = []
         for j in range(2):
-            xb = part_vec[2 * batch + j].astype(BF16).astype(F32)
+            xb = part_vec[j * half + batch].astype(BF16).astype(F32)
             x_parts += [jnp.where(hit_d, xb[0:1], 0.0), jnp.where(hit_d, xb[1:2], 0.0)]
         xx = mm(jnp.concatenate(x_parts, 0).astype(BF16), pick_w)
         w1, w2 = [], []
@@ -323,7 +341,7 @@
     for i in range(members):
         h_copies.append(send(h_send.at[i], h_recv.at[i], h_ssem.at[i], h_rsem.at[i], (down, source(i))))
 
-    total = s_pair[...]
+    total = s_plane[...]
     for i, copy in enumerate(g_copies):
         copy.wait_recv()
         total = total + s_all[i]
@@ -359,7 +377,7 @@
     points = waves.shape[3]
     n_g = basis.shape[2]
     share = n_g // TEAM
-    n_s = max(members // TEAM - 1, 1)
+    n_s = groups // 4 * (members // TEAM) - 1
     any_space = pl.BlockSpec(memory_space=pl.ANY)
     dma = pltpu.SemaphoreType.DMA
     vmem = pltpu.VMEM
@@ -389,7 +407,7 @@
             vmem((2, share), F32),
             vmem((n_s, 2, share), F32),
             vmem((2, share), F32),
-            vmem((groups - 1, 2, share), F32),
+            vmem((3, 2, share), F32),
             vmem((members, 2, NT), F32),
             vmem((members, 2, NT), F32),
             vmem((2, NT), F32),
@@ -400,7 +418,7 @@
             dma((members,)), dma((members,)),
             dma, dma,
             dma((n_s,)), dma((n_s,)),
-            dma((groups - 1,)), dma((groups - 1,)),
+            dma((3,)), dma((3,)),
             dma((members,)), dma((members,)),
             dma, dma,
         ],

time: 20.5 us -> 24.6 us (1.20)
  Pallas kernels: 19.1 us -> 23.2 us
    pallas_call x1, Pallas kernels: 19.1 us -> 23.2 us  [on_device(): pl.pallas_call(functools.partial(kernel, groups, members, n_g), out_shape...]
where the time goes in v7:
time: 24.6 us; the launch traced here: 24.5 us
  Pallas kernels  23.2 us (94%)
  local copies, waits for them, and re-layouts  1.24 us (5%)
    pallas_call x1, Pallas kernels, on_device(): pl.pallas_call(functools.partial(kernel, groups, members, n_g), out_shape...  23.2 us
    unnamed x1, local copies, waits for them, and re-layouts  1.24 us

profile of v7, /device:TPU:0, one launch (start us, length us, event | category | flops | bytes accessed | tf_op | source)
XLA Modules:
  0.0 24.5 jit_solution(18075336294755540409)
XLA Ops:
  0.0 23.2 %shard_map.73 = f32[1,2,16]{2,1,0:T(2,128)} custom-call(bf16[1,2,8,1024]{3,2,1,0:T(8,128)(2,1)} %waves_h.1, f32[1,2,16]{2,1,0:T(2,128)} %vector_h.1, f32[1,16]{1,0:T(1,128)} %energies_h.1, bf16[2,1024,1536]{2,1,0:T(8,128)(2,1)} %basis_h.1, f32[32,1536]{1,0:T(8,128)} %screening_h.1, f32[1536]{0:T(1024)} %coulomb_h.1, s32[1,32]{1,0:T(1,128)} %qmap_h.1), custom_call_target="tpu_custom_call" | custom-call | tf_op jit(solution)/shard_map/pallas_call | solution.py:385
  23.2 1.2 %copy.9 = f32[1,2,16]{2,1,0:T(2,128)} copy(f32[1,2,16]{2,1,0:T(2,128)} %shard_map.73) | data formatting | bytes 256

commit v8 on v6

--- a/solution.py
+++ b/solution.py
@@ -51,8 +51,8 @@
 def kernel(
     groups, members, n_g,
     waves_h, vector_h, energies_h, basis_h, screening_h, coulomb_h, qmap_h, out,
-    energies, coulomb, qmap, basis, screening, team, team_vec, part, part_vec,
-    left, weights, weights_in, own_p, pair_a, pair_b, own_d, s_own, s_in, s_pair, s_all, h_send, h_recv, t_send, t_recv,
+    energies, coulomb, qmap, basis, basis_o, screening, team, team_vec, part, part_vec,
+    left, weights, weights_in, own_p, pair_a, pair_b, own_d, s_own, s_in, s_plane, s_all, h_send, h_recv, t_send, t_recv,
     small_sem, basis_sem, screen_sem, t_ssem, t_rsem, tv_ssem, tv_rsem, p_ssem, p_rsem, pv_ssem, pv_rsem,
     w_ssem, w_rsem, s_ssem, s_rsem, g_ssem, g_rsem, h_ssem, h_rsem, d_ssem, d_rsem,
 ):
@@ -78,11 +78,16 @@
     def group_at(dg):
         return (lax.rem(grp + dg, groups), kin)
 
+    def spot_at(ds, dk):
+        level = lax.div(grp, offset)
+        return kin_at(level * offset + lax.rem(grp - level * offset + ds, offset), dk)
+
     def kin_at(g, dk):
         return (g, lax.rem(kin + dk, members))
 
-    greet = [kin_at(g, dk) for g in (up, down) for dk in range(1, members)]
-    greet += [group_at(dg) for dg in range(1, groups)] + [kin_at(grp, dk) for dk in range(1, members)]
+    plane = [(ds, dk) for ds in range(offset) for dk in range(members) if (ds, dk) != (0, 0)]
+    plane_at = [spot_at(ds, dk) for ds, dk in plane]
+    greet = [kin_at(g, dk) for g in (up, down) for dk in range(members)] + [group_at(2 * offset)] + plane_at
     barrier = pltpu.get_barrier_semaphore()
     for target in greet:
         pl.semaphore_signal(barrier, inc=1, device_id=target, device_id_type=MESH)
@@ -97,10 +102,10 @@
         small.append(pltpu.make_async_copy(src, dst, small_sem.at[i]))
         small[-1].start()
     basis_in = []
-    for n in range(n_chunk):
-        src = pl.ds(pl.multiple_of(rank * share + n * CHUNK, 128), CHUNK)
-        basis_in.append(pltpu.make_async_copy(
-            basis_h.at[:, :, src], basis.at[:, :, pl.ds(n * CHUNK, CHUNK)], basis_sem.at[n]))
+    starts = [pl.multiple_of(r * share + n * CHUNK, 128) for r in (rank, 1 - rank) for n in range(n_chunk)]
+    for n, start in enumerate(starts):
+        dst = (basis if n < n_chunk else basis_o).at[:, :, pl.ds(n % n_chunk * CHUNK, CHUNK)]
+        basis_in.append(pltpu.make_async_copy(basis_h.at[:, :, pl.ds(start, CHUNK)], dst, basis_sem.at[n]))
         basis_in[-1].start()
         if n == 0:
             screen_in = pltpu.make_async_copy(screening_h, screening, screen_sem)
@@ -120,9 +125,9 @@
     one = pl.ds(1, 1)
     targets = [kin_at(up, 2 * i) for i in range(half)]
     targets += [(up, lax.rem(sib + 2 * i, members)) for i in range(half)]
-    part_in = []
     team_in = send(waves_h, team.at[one], t_ssem, t_rsem, (grp, sib))
     team_vec_in = send(vector_h, team_vec.at[one], tv_ssem, tv_rsem, (grp, sib))
+    part_in = []
     for i, target in enumerate(targets):
         part_in.append(send(waves_h, part.at[pl.ds(i, 1)], p_ssem.at[i], p_rsem.at[i], target))
     vec_in = []
@@ -144,18 +149,17 @@
             lim = jnp.where(low_half, wim[2 * h:2 * h + 1], wim[2 * h + 1:2 * h + 2])
             left[s, h, 0] = lre
             left[s, h, 1] = lim
-            if h < 2:
+            if s == 0 and h < 2:
                 pre, pim = conj_mul(lre, lim, cre, cim)
                 res.append(pre)
                 ims.append(pim)
-        pre = jnp.concatenate(res, 0)
-        pim = jnp.concatenate(ims, 0)
-        r0 = s * NT
-        r1 = TEAM * NT + s * NT
-        own_p[r0:r0 + NT, 0:points] = pre.astype(BF16)
-        own_p[r0:r0 + NT, points:] = (-pim).astype(BF16)
-        own_p[r1:r1 + NT, 0:points] = pim.astype(BF16)
-        own_p[r1:r1 + NT, points:] = pre.astype(BF16)
+        if s == 0:
+            pre = jnp.concatenate(res, 0)
+            pim = jnp.concatenate(ims, 0)
+            own_p[0:NT, 0:points] = pre.astype(BF16)
+            own_p[0:NT, points:] = (-pim).astype(BF16)
+            own_p[NT:2 * NT, 0:points] = pim.astype(BF16)
+            own_p[NT:2 * NT, points:] = pre.astype(BF16)
 
     team_part(0)
 
@@ -178,31 +182,31 @@
     weight_in = send(weights.at[:, sib_cols], weights_in.at[1], w_ssem, w_rsem, (grp, sib))
     weights_in[0] = weights[:, my_cols]
 
+    def vector_of(ref):
+        x = ref.astype(BF16).astype(F32)
+        return x[0:1], x[1:2]
+
+    xr, xi = vector_of(team_vec[0])
+    x_rows = jnp.concatenate(
+        [jnp.concatenate([xr, -xi], 1), jnp.concatenate([xi, xr], 1), jnp.zeros((6, 2 * NT), F32)], 0
+    ).astype(BF16)
+
+    def basis_cols(n, ref):
+        return ref[:, :, n * CHUNK:(n + 1) * CHUNK].reshape(2 * points, CHUNK)
+
+    for n, start in enumerate(starts):
+        basis_in[n].wait()
+        dens = mm(own_p[...], basis_cols(n % n_chunk, basis if n < n_chunk else basis_o)).astype(BF16)
+        own_d[:, pl.ds(start, CHUNK)] = dens
+        s_own[:, pl.ds(start, CHUNK)] = mm(x_rows, dens)[0:2]
+    s_copies = []
+    for i, target in enumerate(plane_at):
+        s_copies.append(send(s_own, s_in.at[i], s_ssem.at[i], s_rsem.at[i], target))
+
     team_in.wait_recv()
     team_vec_in.wait_recv()
     team_part(1)
-    xs = []
-    for s in range(TEAM):
-        x = team_vec[s].astype(BF16).astype(F32)
-        xs.append((x[0:1], x[1:2]))
-    xr = jnp.concatenate([x[0] for x in xs], 1)
-    xi = jnp.concatenate([x[1] for x in xs], 1)
-    x_rows = jnp.concatenate(
-        [jnp.concatenate([xr, -xi], 1), jnp.concatenate([xi, xr], 1), jnp.zeros((6, 2 * TEAM * NT), F32)], 0
-    ).astype(BF16)
-
-    def basis_cols(n):
-        return basis[:, :, n * CHUNK:(n + 1) * CHUNK].reshape(2 * points, CHUNK)
-
-    for n in range(n_chunk):
-        basis_in[n].wait()
-        cols = slice(n * CHUNK, (n + 1) * CHUNK)
-        dens = mm(own_p[...], basis_cols(n)).astype(BF16)
-        own_d[:, cols] = dens
-        s_own[:, cols] = mm(x_rows, dens)[0:2]
-    s_copies = []
-    for i in range(teams - 1):
-        s_copies.append(send(s_own, s_in.at[i], s_ssem.at[i], s_rsem.at[i], kin_at(grp, TEAM * (i + 1))))
+    xs = [(xr, xi), vector_of(team_vec[1])]
 
     a_re, a_im = [], []
     for s in range(TEAM):
@@ -242,7 +246,7 @@
         total = None
         for n in range(n_chunk):
             cols = slice(n * CHUNK, (n + 1) * CHUNK)
-            dens = mm(pair_p[...], basis_cols(n)).astype(BF16)
+            dens = mm(pair_p[...], basis_cols(n, basis)).astype(BF16)
             rows = []
             for j in range(2):
                 b = source(2 * batch + j)
@@ -254,29 +258,29 @@
         return jnp.where(same, total, 0.0)
 
     weight_in.wait_recv()
-    for copy in part_in + vec_in:
-        copy.wait_recv()
     pairs_of = (pair_a, pair_b)
 
     def both_products(batch):
         for j in range(2):
+            part_in[2 * batch + j].wait_recv()
+        for j in range(2):
             products(2 * batch + j, pairs_of[batch % 2], j)
 
     both_products(0)
+    kerns = [kernel_of(0, pairs_of[0])]
     total = s_own[...]
     for i, copy in enumerate(s_copies):
         copy.wait_recv()
         total = total + s_in[i]
-    s_pair[...] = total
+    s_plane[...] = total
     g_copies = []
-    for i in range(groups - 1):
-        g_copies.append(send(s_pair, s_all.at[i], g_ssem.at[i], g_rsem.at[i], group_at(i + 1)))
-
-    kerns = []
-    for batch in range(half):
-        if batch + 1 < half:
-            both_products(batch + 1)
+    for i in range(3):
+        g_copies.append(send(s_plane, s_all.at[i], g_ssem.at[i], g_rsem.at[i], group_at(offset * (i + 1))))
+    for batch in range(1, half):
+        both_products(batch)
         kerns.append(kernel_of(batch, pairs_of[batch % 2]))
+    for copy in vec_in:
+        copy.wait_recv()
 
     h_rows = []
     for kern in kerns:
@@ -323,33 +327,32 @@
     for i in range(members):
         h_copies.append(send(h_send.at[i], h_recv.at[i], h_ssem.at[i], h_rsem.at[i], (down, source(i))))
 
-    total = s_pair[...]
+    scale = 1.0 / n_k
+    sums = []
+    for s in range(TEAM):
+        sums.append(jnp.concatenate(
+            [jnp.sum(d_sums[r:r + NT], 0, keepdims=True) for r in (s * NT, n_d + s * NT)], 0))
+    t_send[...] = sums[1]
+    d_copy = send(t_send, t_recv, d_ssem, d_rsem, (grp, sib))
+
+    total = s_plane[...]
     for i, copy in enumerate(g_copies):
         copy.wait_recv()
         total = total + s_all[i]
-    pot = coulomb[my_cols].reshape(1, share) * total
-    ex = mm_nt(jnp.concatenate([hi_lo(pot), jnp.zeros((4, share), BF16)], 0), own_d[...])
+    pot = coulomb[...].reshape(1, n_g) * total
+    ex = mm_nt(jnp.concatenate([hi_lo(pot), jnp.zeros((4, n_g), BF16)], 0), own_d[...])
     ex = ex[0:2] + ex[2:4]
-    exchange = jnp.concatenate([ex[0:1, 0:n_d] + ex[1:2, n_d:], ex[1:2, 0:n_d] - ex[0:1, n_d:]], 0)
-
-    scale = 1.0 / n_k
-    sums = []
-    for s in range(TEAM):
-        direct = jnp.concatenate(
-            [jnp.sum(d_sums[r:r + NT], 0, keepdims=True) for r in (s * NT, n_d + s * NT)], 0)
-        sums.append((2.0 * scale) * exchange[:, s * NT:(s + 1) * NT] - scale * direct)
-    t_send[...] = sums[1]
-    d_copy = send(t_send, t_recv, d_ssem, d_rsem, (grp, sib))
-    result = energies[...] * team_vec[0] + sums[0]
+    exchange = jnp.concatenate([ex[0:1, 0:NT] + ex[1:2, NT:], ex[1:2, 0:NT] - ex[0:1, NT:]], 0)
+    result = energies[...] * team_vec[0] + (2.0 * scale) * exchange
     for copy in started:
         copy.wait_send()
     for copy in h_copies:
         copy.wait_recv()
-    back = h_recv[0]
+    back = sums[0] + h_recv[0]
     for i in range(1, members):
         back = back + h_recv[i]
     d_copy.wait_recv()
-    out[0] = result + t_recv[...] - scale * back
+    out[0] = result - scale * (back + t_recv[...])
 
 
 def on_device(waves, vector, energies, basis, screening, coulomb, qmap):
@@ -359,11 +362,11 @@
     points = waves.shape[3]
     n_g = basis.shape[2]
     share = n_g // TEAM
-    n_s = max(members // TEAM - 1, 1)
+    n_s = groups // 4 * members - 1
     any_space = pl.BlockSpec(memory_space=pl.ANY)
     dma = pltpu.SemaphoreType.DMA
     vmem = pltpu.VMEM
-    n_own = 2 * TEAM * NT
+    n_own = 2 * NT
     return pl.pallas_call(
         functools.partial(kernel, groups, members, n_g),
         out_shape=jax.ShapeDtypeStruct(vector.shape, F32),
@@ -373,6 +376,7 @@
             vmem(energies.shape, F32),
             vmem(coulomb.shape, F32),
             pltpu.SMEM(qmap.shape, jnp.int32),
+            vmem((2, points, share), BF16),
             vmem((2, points, share), BF16),
             vmem(screening.shape, F32),
             vmem((TEAM,) + waves.shape[1:], BF16),
@@ -385,22 +389,22 @@
             vmem((n_own, 2 * points), BF16),
             vmem((4 * ROWS, 2 * points), BF16),
             vmem((4 * ROWS, 2 * points), BF16),
-            vmem((n_own, share), BF16),
-            vmem((2, share), F32),
-            vmem((n_s, 2, share), F32),
-            vmem((2, share), F32),
-            vmem((groups - 1, 2, share), F32),
+            vmem((n_own, n_g), BF16),
+            vmem((2, n_g), F32),
+            vmem((n_s, 2, n_g), F32),
+            vmem((2, n_g), F32),
+            vmem((3, 2, n_g), F32),
             vmem((members, 2, NT), F32),
             vmem((members, 2, NT), F32),
             vmem((2, NT), F32),
             vmem((2, NT), F32),
-            dma((5,)), dma((share // CHUNK,)), dma,
+            dma((5,)), dma((n_g // CHUNK,)), dma,
             dma, dma, dma, dma,
             dma((members,)), dma((members,)),
             dma((members,)), dma((members,)),
             dma, dma,
             dma((n_s,)), dma((n_s,)),
-            dma((groups - 1,)), dma((groups - 1,)),
+            dma((3,)), dma((3,)),
             dma((members,)), dma((members,)),
             dma, dma,
         ],

time: 20.5 us -> 20.1 us (0.980)
  Pallas kernels: 19.1 us -> 18.7 us
    pallas_call x1, Pallas kernels: 19.1 us -> 18.7 us  [on_device(): pl.pallas_call(functools.partial(kernel, groups, members, n_g), out_shape...]
where the time goes in v8:
time: 20.1 us; the launch traced here: 20 us
  Pallas kernels  18.7 us (93%)
  local copies, waits for them, and re-layouts  1.24 us (6%)
    pallas_call x1, Pallas kernels, on_device(): pl.pallas_call(functools.partial(kernel, groups, members, n_g), out_shape...  18.7 us
    unnamed x1, local copies, waits for them, and re-layouts  1.24 us

profile of v8, /device:TPU:0, one launch (start us, length us, event | category | flops | bytes accessed | tf_op | source)
XLA Modules:
  0.0 20.0 jit_solution(10258127928336406657)
XLA Ops:
  0.0 18.7 %shard_map.73 = f32[1,2,16]{2,1,0:T(2,128)} custom-call(bf16[1,2,8,1024]{3,2,1,0:T(8,128)(2,1)} %waves_h.1, f32[1,2,16]{2,1,0:T(2,128)} %vector_h.1, f32[1,16]{1,0:T(1,128)} %energies_h.1, bf16[2,1024,1536]{2,1,0:T(8,128)(2,1)} %basis_h.1, f32[32,1536]{1,0:T(8,128)} %screening_h.1, f32[1536]{0:T(1024)} %coulomb_h.1, s32[1,32]{1,0:T(1,128)} %qmap_h.1), custom_call_target="tpu_custom_call" | custom-call | tf_op jit(solution)/shard_map/pallas_call | solution.py:370
  18.7 1.2 %copy.9 = f32[1,2,16]{2,1,0:T(2,128)} copy(f32[1,2,16]{2,1,0:T(2,128)} %shard_map.73) | data formatting | bytes 256

commit v9 on v5

--- a/solution.py
+++ b/solution.py
@@ -52,7 +52,7 @@
     groups, members, n_g,
     waves_h, vector_h, energies_h, basis_h, screening_h, coulomb_h, qmap_h, out,
     energies, coulomb, qmap, basis, screening, team, team_vec, part, part_vec,
-    left, weights, weights_in, own_p, pair_p, own_d, s_own, s_in, s_pair, s_all, h_send, h_recv, t_send, t_recv,
+    left, weights, weights_in, own_p, pair_p, own_d, s_own, s_in, s_plane, s_all, h_send, h_recv, t_send, t_recv,
     small_sem, basis_sem, screen_sem, t_ssem, t_rsem, tv_ssem, tv_rsem, p_ssem, p_rsem, pv_ssem, pv_rsem, r_ssem,
     w_ssem, w_rsem, s_ssem, s_rsem, g_ssem, g_rsem, h_ssem, h_rsem, d_ssem, d_rsem,
 ):
@@ -78,11 +78,16 @@
     def group_at(dg):
         return (lax.rem(grp + dg, groups), kin)
 
+    def spot_at(ds, dk):
+        level = lax.div(grp, offset)
+        return kin_at(level * offset + lax.rem(grp - level * offset + ds, offset), dk)
+
     def kin_at(g, dk):
         return (g, lax.rem(kin + dk, members))
 
-    greet = [kin_at(g, dk) for g in (up, down) for dk in range(1, members)]
-    greet += [group_at(dg) for dg in range(1, groups)] + [kin_at(grp, dk) for dk in range(1, members)]
+    plane = [(ds, dt) for ds in range(offset) for dt in range(teams) if (ds, dt) != (0, 0)]
+    plane_at = [spot_at(ds, TEAM * dt) for ds, dt in plane]
+    greet = [kin_at(g, dk) for g in (up, down) for dk in range(members)] + [group_at(2 * offset), (grp, sib)] + plane_at
     barrier = pltpu.get_barrier_semaphore()
     for target in greet:
         pl.semaphore_signal(barrier, inc=1, device_id=target, device_id_type=MESH)
@@ -203,8 +208,8 @@
         own_d[:, cols] = dens
         s_own[:, cols] = mm(x_rows, dens)[0:2]
     s_copies = []
-    for i in range(teams - 1):
-        s_copies.append(send(s_own, s_in.at[i], s_ssem.at[i], s_rsem.at[i], kin_at(grp, TEAM * (i + 1))))
+    for i, target in enumerate(plane_at):
+        s_copies.append(send(s_own, s_in.at[i], s_ssem.at[i], s_rsem.at[i], target))
 
     a_re, a_im = [], []
     for s in range(TEAM):
@@ -266,6 +271,8 @@
             part_in[i].wait_recv()
             if i < half:
                 send(part.at[i], part.at[half + i], r_ssem.at[i], p_rsem.at[half + i], (grp, sib))
+        vec_in[2 * batch].wait_recv()
+        vec_in[2 * batch + 1].wait_recv()
         if batch == 0:
             weight_in.wait_recv()
         for j in range(2):
@@ -276,10 +283,10 @@
             for i, copy in enumerate(s_copies):
                 copy.wait_recv()
                 total = total + s_in[i]
-            s_pair[...] = total
+            s_plane[...] = total
             g_copies = []
-            for i in range(groups - 1):
-                g_copies.append(send(s_pair, s_all.at[i], g_ssem.at[i], g_rsem.at[i], group_at(i + 1)))
+            for i in range(3):
+                g_copies.append(send(s_plane, s_all.at[i], g_ssem.at[i], g_rsem.at[i], group_at(offset * (i + 1))))
 
     h_rows = []
     for kern in kerns:
@@ -299,11 +306,7 @@
     h_copies = []
     for i in range(members):
         h_send[i] = jnp.concatenate([h_row(i // 2, 0, i % 2), h_row(i // 2, 1, i % 2)], 0)
-    for i in range(members):
-        h_copies.append(send(h_send.at[i], h_recv.at[i], h_ssem.at[i], h_rsem.at[i], (down, source(i))))
-
-    for copy in vec_in:
-        copy.wait_recv()
+
     d_re = jnp.zeros((ROWS, side), F32)
     d_im = jnp.zeros((ROWS, side), F32)
     for batch, kern in enumerate(kerns):
@@ -328,7 +331,10 @@
     d_sums = d_sums[0:2 * n_d] + d_sums[2 * n_d:]
     d_sums = jnp.where((iota((2 * n_d, NT), 0) // 4) % 4 == iota((2 * n_d, NT), 1) % 4, d_sums, 0.0)
 
-    total = s_pair[...]
+    for i in range(members):
+        h_copies.append(send(h_send.at[i], h_recv.at[i], h_ssem.at[i], h_rsem.at[i], (down, source(i))))
+
+    total = s_plane[...]
     for i, copy in enumerate(g_copies):
         copy.wait_recv()
         total = total + s_all[i]
@@ -346,6 +352,8 @@
     t_send[...] = sums[1]
     d_copy = send(t_send, t_recv, d_ssem, d_rsem, (grp, sib))
     result = energies[...] * team_vec[0] + sums[0]
+    for copy in started:
+        copy.wait_send()
     for copy in h_copies:
         copy.wait_recv()
     back = h_recv[0]
@@ -354,9 +362,6 @@
     d_copy.wait_recv()
     out[0] = result + t_recv[...] - scale * back
 
-    for copy in started:
-        copy.wait_send()
-
 
 def on_device(waves, vector, energies, basis, screening, coulomb, qmap):
     groups = lax.axis_size("grp")
@@ -365,7 +370,7 @@
     points = waves.shape[3]
     n_g = basis.shape[2]
     share = n_g // TEAM
-    n_s = max(members // TEAM - 1, 1)
+    n_s = groups // 4 * (members // TEAM) - 1
     any_space = pl.BlockSpec(memory_space=pl.ANY)
     dma = pltpu.SemaphoreType.DMA
     vmem = pltpu.VMEM
@@ -394,7 +399,7 @@
             vmem((2, share), F32),
             vmem((n_s, 2, share), F32),
             vmem((2, share), F32),
-            vmem((groups - 1, 2, share), F32),
+            vmem((3, 2, share), F32),
             vmem((members, 2, NT), F32),
             vmem((members, 2, NT), F32),
             vmem((2, NT), F32),
@@ -406,7 +411,7 @@
             dma((half,)),
             dma, dma,
             dma((n_s,)), dma((n_s,)),
-            dma((groups - 1,)), dma((groups - 1,)),
+            dma((3,)), dma((3,)),
             dma((members,)), dma((members,)),
             dma, dma,
         ],

time: 19.1 us -> 19.1 us (level)
  no operation moved by 1% of the time
where the time goes in v9:
time: 19.1 us; the launch traced here: 19 us
  Pallas kernels  17.7 us (93%)
  local copies, waits for them, and re-layouts  1.24 us (6%)
    pallas_call x1, Pallas kernels, on_device(): pl.pallas_call(functools.partial(kernel, groups, members, n_g), out_shape...  17.7 us
    unnamed x1, local copies, waits for them, and re-layouts  1.24 us

profile of v9, /device:TPU:0, one launch (start us, length us, event | category | flops | bytes accessed | tf_op | source)
XLA Modules:
  0.0 19.0 jit_solution(15887726775846810502)
XLA Ops:
  0.0 17.7 %shard_map.73 = f32[1,2,16]{2,1,0:T(2,128)} custom-call(bf16[1,2,8,1024]{3,2,1,0:T(8,128)(2,1)} %waves_h.1, f32[1,2,16]{2,1,0:T(2,128)} %vector_h.1, f32[1,16]{1,0:T(1,128)} %energies_h.1, bf16[2,1024,1536]{2,1,0:T(8,128)(2,1)} %basis_h.1, f32[32,1536]{1,0:T(8,128)} %screening_h.1, f32[1536]{0:T(1024)} %coulomb_h.1, s32[1,32]{1,0:T(1,128)} %qmap_h.1), custom_call_target="tpu_custom_call" | custom-call | tf_op jit(solution)/shard_map/pallas_call | solution.py:378
  17.7 1.2 %copy.9 = f32[1,2,16]{2,1,0:T(2,128)} copy(f32[1,2,16]{2,1,0:T(2,128)} %shard_map.73) | data formatting | bytes 256

commit v10 on v9

--- a/solution.py
+++ b/solution.py
@@ -202,6 +202,10 @@
         return basis[:, :, n * CHUNK:(n + 1) * CHUNK].reshape(2 * points, CHUNK)
 
     for n in range(n_chunk):
+        if n == n_chunk - 1:
+            for i in range(half):
+                part_in[i].wait_recv()
+                send(part.at[i], part.at[half + i], r_ssem.at[i], p_rsem.at[half + i], (grp, sib))
         basis_in[n].wait()
         cols = slice(n * CHUNK, (n + 1) * CHUNK)
         dens = mm(own_p[...], basis_cols(n)).astype(BF16)
@@ -268,9 +272,7 @@
                 part_in[i] = pltpu.make_async_remote_copy(
                     src_ref=part.at[k], dst_ref=part.at[k], send_sem=r_ssem.at[i - half], recv_sem=p_rsem.at[i],
                     device_id=(grp, sib), device_id_type=MESH)
-            part_in[i].wait_recv()
-            if i < half:
-                send(part.at[i], part.at[half + i], r_ssem.at[i], p_rsem.at[half + i], (grp, sib))
+                part_in[i].wait_recv()
         vec_in[2 * batch].wait_recv()
         vec_in[2 * batch + 1].wait_recv()
         if batch == 0:

time: 19.1 us -> 21.1 us (1.10)
  Pallas kernels: 17.7 us -> 19.7 us
    pallas_call x1, Pallas kernels: 17.7 us -> 19.7 us  [on_device(): pl.pallas_call(functools.partial(kernel, groups, members, n_g), out_shape...]
where the time goes in v10:
time: 21.1 us; the launch traced here: 20.9 us
  Pallas kernels  19.7 us (93%)
  local copies, waits for them, and re-layouts  1.24 us (6%)
    pallas_call x1, Pallas kernels, on_device(): pl.pallas_call(functools.partial(kernel, groups, members, n_g), out_shape...  19.7 us
    unnamed x1, local copies, waits for them, and re-layouts  1.24 us

profile of v10, /device:TPU:0, one launch (start us, length us, event | category | flops | bytes accessed | tf_op | source)
XLA Modules:
  0.0 20.9 jit_solution(8672693120519116922)
XLA Ops:
  0.0 19.7 %shard_map.73 = f32[1,2,16]{2,1,0:T(2,128)} custom-call(bf16[1,2,8,1024]{3,2,1,0:T(8,128)(2,1)} %waves_h.1, f32[1,2,16]{2,1,0:T(2,128)} %vector_h.1, f32[1,16]{1,0:T(1,128)} %energies_h.1, bf16[2,1024,1536]{2,1,0:T(8,128)(2,1)} %basis_h.1, f32[32,1536]{1,0:T(8,128)} %screening_h.1, f32[1536]{0:T(1024)} %coulomb_h.1, s32[1,32]{1,0:T(1,128)} %qmap_h.1), custom_call_target="tpu_custom_call" | custom-call | tf_op jit(solution)/shard_map/pallas_call | solution.py:380
  19.7 1.2 %copy.9 = f32[1,2,16]{2,1,0:T(2,128)} copy(f32[1,2,16]{2,1,0:T(2,128)} %shard_map.73) | data formatting | bytes 256

commit v11 on v5

--- a/solution.py
+++ b/solution.py
@@ -270,8 +270,7 @@
             weight_in.wait_recv()
         for j in range(2):
             products(2 * batch + j, batch % 2, j)
-        kerns.append(kernel_of(batch))
-        if batch == 0:
+        if batch == 1:
             total = s_own[...]
             for i, copy in enumerate(s_copies):
                 copy.wait_recv()
@@ -280,6 +279,7 @@
             g_copies = []
             for i in range(groups - 1):
                 g_copies.append(send(s_pair, s_all.at[i], g_ssem.at[i], g_rsem.at[i], group_at(i + 1)))
+        kerns.append(kernel_of(batch))
 
     h_rows = []
     for kern in kerns:

time: 19.1 us -> 19.3 us (1.010)
  Pallas kernels: 17.7 us -> 17.9 us
where the time goes in v11:
time: 19.3 us; the launch traced here: 19.1 us
  Pallas kernels  17.9 us (93%)
  local copies, waits for them, and re-layouts  1.24 us (6%)
    pallas_call x1, Pallas kernels, on_device(): pl.pallas_call(functools.partial(kernel, groups, members, n_g), out_shape...  17.9 us
    unnamed x1, local copies, waits for them, and re-layouts  1.24 us

profile of v11, /device:TPU:0, one launch (start us, length us, event | category | flops | bytes accessed | tf_op | source)
XLA Modules:
  0.0 19.1 jit_solution(11585003790271792676)
XLA Ops:
  0.0 17.9 %shard_map.73 = f32[1,2,16]{2,1,0:T(2,128)} custom-call(bf16[1,2,8,1024]{3,2,1,0:T(8,128)(2,1)} %waves_h.1, f32[1,2,16]{2,1,0:T(2,128)} %vector_h.1, f32[1,16]{1,0:T(1,128)} %energies_h.1, bf16[2,1024,1536]{2,1,0:T(8,128)(2,1)} %basis_h.1, f32[32,1536]{1,0:T(8,128)} %screening_h.1, f32[1536]{0:T(1024)} %coulomb_h.1, s32[1,32]{1,0:T(1,128)} %qmap_h.1), custom_call_target="tpu_custom_call" | custom-call | tf_op jit(solution)/shard_map/pallas_call | solution.py:373
  17.9 1.2 %copy.9 = f32[1,2,16]{2,1,0:T(2,128)} copy(f32[1,2,16]{2,1,0:T(2,128)} %shard_map.73) | data formatting | bytes 256
